TPU v7x, 256 devices: a whole 4x4x8 slice. The times are simulated.
256 devices in a mesh: pipe: 8 (over y, core), tensor: 16 (over x, z_hi), dp: 2 (over z_lo).
Axes of the slice: x: 4, y: 4, z: 8 (z_hi: 4, z_lo: 2; z = z_hi * 2 + z_lo), core: 2. Of those that a mesh axis runs over, the one named last changes fastest.
Arguments:
- hidden: bfloat16 [8, 2, 512, 8192], P('pipe', None, 'dp', 'tensor'), may hold values from -6 to 6
- query_weight: bfloat16 [8, 2, 8192, 4096], P('pipe', None, 'dp', 'tensor'), as said below
- keyval_weight: bfloat16 [8, 2, 8192, 1024], P('pipe', None, 'dp', 'tensor'), as said below
- doc_ids: int32 [8, 2, 2, 256], P('pipe', None, 'dp'), may hold values from 0 to 3, never falling along the last dimension, each value on 1 to 128 neighbouring positions
- cotangent: bfloat16 [8, 2, 512, 4096], P('pipe', None, 'dp', 'tensor'), may hold values from -6 to 6
Outputs:
- attended: bfloat16 [8, 2, 512, 4096], P('pipe', None, 'dp', 'tensor')
- hidden_grad: bfloat16 [8, 2, 512, 8192], P('pipe', None, 'dp', 'tensor')
- query_grad: float32 [8, 8192, 4096], P('pipe', 'dp', 'tensor')
- slab_keyvalue_gradient: float32 [8, 8192, 1024], P('pipe', 'dp', 'tensor')
Inputs may be any that keep to these rules, and one draw needn't show every extreme that they name: `doc_ids`: along the last dimension ids never fall; each document holds 1 to 128 tokens, one exactly 128. query_weight[p, 1] equals query_weight[7 - p, 0] for every p. keyval_weight[p, 1] equals keyval_weight[7 - p, 0] for every p.
All inputs are finite; a program needn't handle non-finite values.
Results may differ from a plain program's by a relative error of at most 0.025.
Values may be sent and summed in bfloat16 or wider, within the bound.
A program may use at most 128 MiB of HBM per device.

v0:
```python
import jax
import jax.numpy as jnp
from jax import lax
from jax.sharding import PartitionSpec as P

KEYVALUE_HEADS = 4
HEAD_SIZE = 128


def from_partner(value, axis, apart):
    mask = 2**apart
    pairs = [(source, source ^ mask) for source in range(lax.axis_size(axis))]
    return lax.ppermute(value, axis, pairs)


def tables(sequence_length):
    positions = jnp.arange(sequence_length, dtype=jnp.float32)
    freqs = 10000.0 ** (-2.0 * jnp.arange(HEAD_SIZE // 2, dtype=jnp.float32) / HEAD_SIZE)
    angles = positions[:, None] * freqs[None, :]
    return (jnp.cos(angles), jnp.sin(angles))


def rotate(values, cosine_table, sine_table):
    half_width = values.shape[-1] // 2
    first, second = (values[..., :half_width], values[..., half_width:])
    return jnp.concatenate(
        [first * cosine_table - second * sine_table, second * cosine_table + first * sine_table], -1
    )


def inverse_rotation(values, cosine_table, sine_table):
    half_width = values.shape[-1] // 2
    first, second = (values[..., :half_width], values[..., half_width:])
    return jnp.concatenate(
        [first * cosine_table + second * sine_table, second * cosine_table - first * sine_table], -1
    )


def body(hidden, query_weight, keyval_weight, doc_ids, cotangent):
    tensor_group_count = lax.axis_size("tensor")
    query_group_width = tensor_group_count // KEYVALUE_HEADS
    group_bits = query_group_width.bit_length() - 1
    pipe_bits = lax.axis_size("pipe").bit_length() - 1
    tensor_rank = lax.axis_index("tensor")
    score_scale = HEAD_SIZE ** (-0.5)
    input_rows = lax.all_gather(hidden[0], "tensor", axis=2, tiled=True)
    sequence_length = input_rows.shape[1]
    query_pieces, keyvalue_pieces = (
        lax.all_gather(query_weight[0], "dp", axis=1, tiled=True),
        lax.all_gather(keyval_weight[0], "dp", axis=1, tiled=True),
    )
    cosine_table, sine_table = tables(sequence_length)
    heads_local = query_weight.shape[3] // HEAD_SIZE
    projected_rows = jnp.einsum(
        "emd,edc->emc", input_rows, query_pieces, preferred_element_type=jnp.float32
    )
    projected_rows = projected_rows.reshape(2, sequence_length, heads_local, HEAD_SIZE)
    queries = rotate(projected_rows, cosine_table[None, :, None], sine_table[None, :, None]).astype(
        jnp.bfloat16
    )
    shared = jnp.einsum(
        "emd,edc->emc", input_rows, keyvalue_pieces, preferred_element_type=jnp.float32
    )
    for bit_pos in range(group_bits):
        received = from_partner(shared.astype(jnp.bfloat16), "tensor", bit_pos).astype(shared.dtype)
        upper_half = tensor_rank >> bit_pos & 1 == 1
        shared = jnp.where(
            upper_half,
            jnp.concatenate([received, shared], -1),
            jnp.concatenate([shared, received], -1),
        )
    keys = rotate(shared[..., :HEAD_SIZE], cosine_table[None], sine_table[None]).astype(
        jnp.bfloat16
    )
    values = shared[..., HEAD_SIZE:].astype(jnp.bfloat16)
    scores = (
        jnp.einsum("emhd,ekd->ehmk", queries, keys, preferred_element_type=jnp.float32)
        * score_scale
    )
    doc_rows = doc_ids[0, :, 0, :]
    token_index = jnp.arange(sequence_length)
    causal = (token_index[None, :] <= token_index[:, None])[None]
    allowed = causal & (doc_rows[:, :, None] == doc_rows[:, None, :])
    weights = jnp.where(allowed[:, None], jnp.exp(scores), 0.0)
    probs_full = weights / jnp.sum(weights, axis=-1, keepdims=True)
    probs_low = probs_full.astype(jnp.bfloat16)
    attended = jnp.einsum("ehmk,ekd->emhd", probs_low, values, preferred_element_type=jnp.float32)
    attended = attended.astype(jnp.bfloat16).reshape(2, sequence_length, heads_local * HEAD_SIZE)
    grad_out = cotangent[0].reshape(2, sequence_length, heads_local, HEAD_SIZE)
    value_gradient = jnp.einsum(
        "ehmk,emhd->ekd", probs_low, grad_out, preferred_element_type=jnp.float32
    )
    grad_probs = jnp.einsum("emhd,ekd->ehmk", grad_out, values, preferred_element_type=jnp.float32)
    row_dot = jnp.sum(grad_probs * probs_full, axis=-1, keepdims=True)
    grad_scores = (probs_full * (grad_probs - row_dot) * score_scale).astype(jnp.bfloat16)
    query_gradient = jnp.einsum(
        "ehmk,ekd->emhd", grad_scores, keys, preferred_element_type=jnp.float32
    )
    query_gradient = inverse_rotation(
        query_gradient, cosine_table[None, :, None], sine_table[None, :, None]
    )
    query_gradient = query_gradient.astype(jnp.bfloat16).reshape(
        2, sequence_length, heads_local * HEAD_SIZE
    )
    key_gradient = jnp.einsum(
        "ehmk,emhd->ekd", grad_scores, queries, preferred_element_type=jnp.float32
    )
    key_gradient = inverse_rotation(key_gradient, cosine_table[None], sine_table[None])
    partial_sum = jnp.concatenate([key_gradient, value_gradient], -1)
    for bit_pos in reversed(range(group_bits)):
        half_width = partial_sum.shape[-1] // 2
        upper_half = tensor_rank >> bit_pos & 1 == 1
        kept_half = jnp.where(
            upper_half, partial_sum[..., half_width:], partial_sum[..., :half_width]
        )
        sent_half = jnp.where(
            upper_half, partial_sum[..., :half_width], partial_sum[..., half_width:]
        )
        partial_sum = kept_half + from_partner(
            sent_half.astype(jnp.bfloat16), "tensor", bit_pos
        ).astype(sent_half.dtype)
    keyvalue_gradient = partial_sum.astype(jnp.bfloat16)
    row_term = jnp.einsum(
        "hpi,hgi->ghp", query_gradient, query_pieces, preferred_element_type=jnp.float32
    )
    summed = lax.psum_scatter(
        (
            row_term
            + jnp.einsum(
                "hpi,hgi->ghp",
                keyvalue_gradient,
                keyvalue_pieces,
                preferred_element_type=jnp.float32,
            )
        ).astype(jnp.bfloat16),
        "tensor",
        scatter_dimension=0,
        tiled=True,
    ).astype(jnp.float32)
    hidden_grad = jnp.transpose(summed, (1, 2, 0)).astype(jnp.bfloat16)[None]
    query_parts = jnp.einsum(
        "emd,emc->edc", input_rows, query_gradient, preferred_element_type=jnp.float32
    ).astype(jnp.bfloat16)
    keyval_parts = jnp.einsum(
        "emd,emc->edc", input_rows, keyvalue_gradient, preferred_element_type=jnp.float32
    ).astype(jnp.bfloat16)
    scattered_query, scattered_keyval = (
        lax.psum_scatter(
            query_parts.astype(jnp.float32).astype(jnp.bfloat16),
            "dp",
            scatter_dimension=1,
            tiled=True,
        ).astype(jnp.float32),
        lax.psum_scatter(
            keyval_parts.astype(jnp.float32).astype(jnp.bfloat16),
            "dp",
            scatter_dimension=1,
            tiled=True,
        ).astype(jnp.float32),
    )
    moving = (scattered_query[1], scattered_keyval[1])
    for bit_pos in range(pipe_bits):
        moving = (
            from_partner(moving[0].astype(jnp.bfloat16), "pipe", bit_pos).astype(jnp.float32),
            from_partner(moving[1].astype(jnp.bfloat16), "pipe", bit_pos).astype(jnp.float32),
        )
    query_grad = scattered_query[0] + moving[0]
    slab_keyvalue_gradient = scattered_keyval[0] + moving[1]
    return (attended[None], hidden_grad, query_grad[None], slab_keyvalue_gradient[None])


def solution(mesh):
    in_specs = (
        P("pipe", None, "dp", "tensor"),
        P("pipe", None, "dp", "tensor"),
        P("pipe", None, "dp", "tensor"),
        P("pipe", None, "dp", None),
        P("pipe", None, "dp", "tensor"),
    )
    out_specs = (
        P("pipe", None, "dp", "tensor"),
        P("pipe", None, "dp", "tensor"),
        P("pipe", "dp", "tensor"),
        P("pipe", "dp", "tensor"),
    )
    return jax.shard_map(body, mesh=mesh, in_specs=in_specs, out_specs=out_specs, check_vma=False)
```

profile of v0, /device:TPU:31, one launch (start us, length us, event | category | flops | bytes accessed | tf_op | source)
XLA Modules:
  0.0 601.3 jit_solution(4895637535661759283)
XLA Ops:
  7.2 0.0 all-gather.9.cloned.1.call-start
  7.2 0.7 all-gather.9.cloned.1.call-update
  7.9 0.0 all-gather.7.cloned.1.call-start
  8.0 0.7 all-gather.7.cloned.1.call-update
  8.7 0.0 all-gather.11.cloned.1.call-start
  8.7 6.3 %copy.28 = bf16[1,2,4096,256]{2,3,1,0:T(8,128)(2,1)} copy(bf16[1,2,4096,256]{3,2,1,0:T(8,128)(2,1)} %param.6) | data formatting | bytes 8388608 | tf_op args[1]
  15.1 0.0 reduce-scatter.6.cloned.1.call-start
  15.2 0.3 fusion.37
  15.5 0.1 copy.30
  15.6 0.1 copy.32
  15.7 0.1 copy.69
  15.9 0.2 compare_and_fusion
  16.0 34.7 %all-gather.9.cloned.1.call-done = bf16[1,2,8192,64]{2,3,1,0:T(8,128)(2,1)} async-done(((bf16[1,2,4096,64]{2,3,1,0:T(8,128)(2,1)}), bf16[1,2,8192,64]{2,3,1,0:T(8,128)(2,1)}) %all-gather.9.cloned.1.call-update) | async-done | bytes 2097168 | tf_op jit(solution)/shard_map/all_gather | solution.py:50
  50.8 127.2 %all-gather.7.cloned.1.call-done = bf16[1,2,256,8192]{3,2,1,0:T(8,128)(2,1)} async-done(((bf16[1,2,256,512]{3,2,1,0:T(8,128)(2,1)}), bf16[1,2,256,8192]{3,2,1,0:T(8,128)(2,1)}) %all-gather.7.cloned.1.call-update) | async-done | bytes 8388624 | tf_op jit(solution)/shard_map/all_gather | solution.py:46
  177.9 6.6 %fusion.53 = (bf16[2,256,64]{1,2,0:T(8,128)(2,1)S(1)}, f32[2,256,64]{1,2,0:T(8,128)S(1)}) fusion(bf16[1,2,8192,64]{2,3,1,0:T(8,128)(2,1)} %all-gather.9.cloned.1.call-done, bf16[1,2,256,8192]{3,2,1,0:T(8,128)(2,1)} %all-gather.7.cloned.1.call-done), kind=kOutput, calls=%fused_computation.86 | convolution fusion | flops 536903680 | bytes 10682368 | tf_op jit(solution)/shard_map/emd,edc->emc/dot_general | solution.py:61
  184.6 1.9 collective-permute-start
  186.4 101.8 %all-gather.11.cloned.1.call-done = bf16[1,2,8192,256]{2,3,1,0:T(8,128)(2,1)} async-done(((bf16[1,2,4096,256]{2,3,1,0:T(8,128)(2,1)}), bf16[1,2,8192,256]{2,3,1,0:T(8,128)(2,1)}) %all-gather.11.cloned.1.call-update) | async-done | bytes 8388624 | tf_op jit(solution)/shard_map/all_gather | solution.py:49
  288.2 8.1 %fusion.6 = f32[2,256,256]{1,2,0:T(8,128)S(1)} fusion(bf16[1,2,8192,256]{2,3,1,0:T(8,128)(2,1)} %all-gather.11.cloned.1.call-done, bf16[1,2,256,8192]{3,2,1,0:T(8,128)(2,1)} %all-gather.7.cloned.1.call-done), kind=kOutput, calls=%fused_computation.9 | convolution fusion | flops 2147483648 | bytes 17301504 | tf_op jit(solution)/shard_map/emd,edc->emc/dot_general | solution.py:54
  296.4 0.2 copy.68
  296.6 0.2 copy.67
  296.8 4.6 collective-permute-start.1
  301.5 0.8 subtract_convert_fusion.1
  302.3 2.9 collective-permute-done.1
  305.3 1.3 convolution_bitcast_fusion
  306.6 1.5 fusion.32
  308.2 2.1 convolution_bitcast_fusion.1
  310.2 0.3 add_convert_fusion.1
  310.5 0.1 pad_maximum_fusion.1
  310.7 0.1 copy.39
  310.8 9.0 %fusion.2 = bf16[2,8192,256]{1,2,0:T(8,128)(2,1)} fusion(bf16[2,256,256]{1,2,0:T(8,128)(2,1)S(1)} %bitcast.105, bf16[1,2,256,8192]{3,2,1,0:T(8,128)(2,1)} %all-gather.7.cloned.1.call-done), kind=kOutput, calls=%fused_computation.4 | convolution fusion | flops 2151677952 | bytes 17039360 | tf_op jit(solution)/shard_map/emd,emc->edc/dot_general | solution.py:141
  319.8 0.0 reduce-scatter.6.cloned.1.call-update
  319.8 0.2 reduce-scatter.8.cloned.1.call-start
  320.0 0.7 copy-done.4
  320.7 0.1 copy-done.5
  320.8 2.1 convolution_bitcast_fusion.2
  323.0 0.3 select_convert_fusion
  323.3 4.8 collective-permute-start.2
  328.0 3.0 collective-permute-done.2
  331.2 8.4 %collective-permute-start.3 = (bf16[2,256,64]{1,2,0:T(8,128)(2,1)S(1)}, bf16[2,256,64]{1,2,0:T(8,128)(2,1)S(1)}, u32[]{:S(2)}, u32[]{:S(2)}) collective-permute-start(bf16[2,256,64]{1,2,0:T(8,128)(2,1)S(1)} %select_convert_fusion.1), channel_id=1, source_target_pairs={{0,2},{2,0},{4,6},{6,4},{8,10},{10,8},{12,14},{14,12},{16,18},{18,... | collective-permute-start | bytes 196616 | tf_op jit(solution)/shard_map/ppermute | solution.py:13
  339.5 2.7 collective-permute-done.3
  342.3 6.3 %fusion.3 = bf16[2,8192,64]{1,2,0:T(8,128)(2,1)} fusion(bf16[2,256,64]{1,2,0:T(8,128)(2,1)S(1)} %add_convert_fusion.3, bf16[1,2,256,8192]{3,2,1,0:T(8,128)(2,1)} %all-gather.7.cloned.1.call-done), kind=kOutput, calls=%fused_computation.6 | convolution fusion | flops 537919488 | bytes 10551296 | tf_op jit(solution)/shard_map/emd,emc->edc/dot_general | solution.py:144
  348.5 0.0 reduce-scatter.8.cloned.1.call-update
  348.6 0.0 reduce-scatter.4.cloned.1.call-start
  348.6 11.9 %fusion.4 = f32[2,256,8192]{2,1,0:T(8,128)} fusion(bf16[2,256,256]{1,2,0:T(8,128)(2,1)S(1)} %bitcast.106, bf16[1,2,8192,256]{2,3,1,0:T(8,128)(2,1)} %all-gather.11.cloned.1.call-done), kind=kOutput, calls=%fused_computation.7 | convolution fusion | flops 2147483648 | bytes 25427968 | tf_op jit(solution)/shard_map/hpi,hgi->ghp/dot_general | solution.py:123
  360.6 11.7 %fusion.1 = bf16[8192,2,256]{0,2,1:T(8,128)(2,1)} fusion(f32[2,256,8192]{2,1,0:T(8,128)} %fusion.4, bf16[2,256,64]{1,2,0:T(8,128)(2,1)S(1)} %add_convert_fusion.3, bf16[1,2,8192,64]{2,3,1,0:T(8,128)(2,1)S(1)} %copy-done), kind=kOutput, calls=%fused_computation.3 | convolution fusion | flops 545259520 | bytes 27328512 | tf_op jit(solution)/shard_map/hpi,hgi->ghp/dot_general | solution.py:129
  372.3 57.7 %reduce-scatter.6.cloned.1.call-done = bf16[2,4096,256]{1,2,0:T(8,128)(2,1)} async-done(((bf16[2,8192,256]{1,2,0:T(8,128)(2,1)}), bf16[2,4096,256]{1,2,0:T(8,128)(2,1)}) %reduce-scatter.6.cloned.1.call-update) | async-done | bytes 4194320 | tf_op jit(solution)/shard_map/reduce_scatter | solution.py:148
  429.9 1.7 slice_bitcast_fusion
  431.7 0.7 collective-permute-start.4
  432.3 3.9 collective-permute-done.4
  436.2 0.6 collective-permute-start.5
  436.8 32.9 %reduce-scatter.8.cloned.1.call-done = bf16[2,4096,64]{1,2,0:T(8,128)(2,1)} async-done(((bf16[2,8192,64]{1,2,0:T(8,128)(2,1)}), bf16[2,4096,64]{1,2,0:T(8,128)(2,1)}) %reduce-scatter.8.cloned.1.call-update) | async-done | bytes 1048592 | tf_op jit(solution)/shard_map/reduce_scatter | solution.py:154
  469.7 1.1 slice_bitcast_fusion.2
  470.8 0.8 collective-permute-start.7
  471.6 11.8 %collective-permute-done.5 = bf16[4096,256]{0,1:T(8,128)(2,1)} collective-permute-done((bf16[4096,256]{0,1:T(8,128)(2,1)}, bf16[4096,256]{0,1:T(8,128)(2,1)}, u32[]{:S(2)}, u32[]{:S(2)}) %collective-permute-start.5) | collective-permute-done | bytes 2097184 | tf_op jit(solution)/shard_map/ppermute | solution.py:13
  483.4 1.1 collective-permute-start.6
  484.6 55.7 %collective-permute-done.8 = bf16[4096,64]{0,1:T(8,128)(2,1)S(1)} collective-permute-done((bf16[4096,64]{0,1:T(8,128)(2,1)S(1)}, bf16[4096,64]{0,1:T(8,128)(2,1)S(1)}, u32[]{:S(2)}, u32[]{:S(2)}) %collective-permute-start.8) | collective-permute-done | bytes 524320 | tf_op jit(solution)/shard_map/ppermute | solution.py:13
  540.2 3.3 collective-permute-start.9
  543.6 0.2 convolution_convert_fusion.2
  543.8 0.8 copy.46
  544.6 9.2 %collective-permute-done.9 = bf16[4096,64]{0,1:T(8,128)(2,1)S(1)} collective-permute-done((bf16[4096,64]{0,1:T(8,128)(2,1)S(1)}, bf16[4096,64]{0,1:T(8,128)(2,1)S(1)}, u32[]{:S(2)}, u32[]{:S(2)}) %collective-permute-start.9) | collective-permute-done | bytes 524320 | tf_op jit(solution)/shard_map/ppermute | solution.py:13
  553.9 2.1 fusion.23
  556.0 4.9 fusion.13
  560.9 5.6 copy.47
  566.5 28.0 %reduce-scatter.4.cloned.1.call-done = bf16[512,2,256]{0,2,1:T(8,128)(2,1)} async-done(((bf16[8192,2,256]{0,2,1:T(8,128)(2,1)}), bf16[512,2,256]{0,2,1:T(8,128)(2,1)}) %reduce-scatter.4.cloned.1.call-update) | async-done | bytes 524304 | tf_op jit(solution)/shard_map/reduce_scatter | solution.py:126
  (33 shorter events, 0.4 us)
Async XLA Ops:
  7.2 8.0 %copy-start.7 = (s32[1,2,1,256]{3,2,1,0:T(1,128)S(1)}, s32[1,2,1,256]{3,2,1,0:T(1,128)}, u32[]{:S(2)}) copy-start(s32[1,2,1,256]{3,2,1,0:T(1,128)} %param.8) | copy-start | bytes 6148
  7.2 8.5 %copy-start.6 = (bf16[1,2,256,256]{3,2,1,0:T(8,128)(2,1)S(1)}, bf16[1,2,256,256]{3,2,1,0:T(8,128)(2,1)}, u32[]{:S(2)}) copy-start(bf16[1,2,256,256]{3,2,1,0:T(8,128)(2,1)} %param.9) | copy-start | bytes 786436
  7.2 43.6 %all-gather.9.cloned.1.call-start = ((), (), s32[]{:S(2)}) async-start(), calls=%async_computation.7 | async-start | bytes 3145728 | tf_op jit(solution)/shard_map/all_gather | solution.py:50
  7.9 170.0 %all-gather.7.cloned.1.call-start = ((), (), s32[]{:S(2)}) async-start(), calls=%async_computation.6 | async-start | bytes 8912896 | tf_op jit(solution)/shard_map/all_gather | solution.py:46
  8.7 279.5 %all-gather.11.cloned.1.call-start = ((), (), s32[]{:S(2)}) async-start(), calls=%async_computation.8 | async-start | bytes 12582912 | tf_op jit(solution)/shard_map/all_gather | solution.py:49
  15.1 414.9 %reduce-scatter.6.cloned.1.call-start = ((), (), s32[]{:S(2)}) async-start(), calls=%async_computation.4 | async-start | bytes 12582912 | tf_op jit(solution)/shard_map/reduce_scatter | solution.py:148
  184.6 112.2 %collective-permute-start = (bf16[2,256,64]{1,2,0:T(8,128)(2,1)S(1)}, bf16[2,256,64]{1,2,0:T(8,128)(2,1)S(1)}, u32[]{:S(2)}, u32[]{:S(2)}) collective-permute-start(bf16[2,256,64]{1,2,0:T(8,128)(2,1)S(1)} %get-tuple-element.26), channel_id=1, source_target_pairs={{0,2},{2,0},{4,6},{6,4},{8,10},{10,8},{12,14},{14,12},{16,18},{18,... | collective-permute-start | bytes 196616 | tf_op jit(solution)/shard_map/ppermute | solution.py:13
  296.8 8.4 %collective-permute-start.1 = (bf16[2,256,128]{1,2,0:T(8,128)(2,1)S(1)}, bf16[2,256,128]{1,2,0:T(8,128)(2,1)S(1)}, u32[]{:S(2)}, u32[]{:S(2)}) collective-permute-start(bf16[2,256,128]{1,2,0:T(8,128)(2,1)S(1)} %get-tuple-element.12), channel_id=1, source_target_pairs={{0,4},{2,6},{4,0},{6,2},{8,12},{10,14},{12,8},{14,10},{16,20},{18,... | collective-permute-start | bytes 393224 | tf_op jit(solution)/shard_map/ppermute | solution.py:13
  302.3 8.2 %copy-start.3 = (bf16[2,256,2,64]{3,1,2,0:T(8,128)(2,1)}, bf16[2,256,2,64]{3,1,2,0:T(8,128)(2,1)S(1)}, u32[]{:S(2)}) copy-start(bf16[2,256,2,64]{3,1,2,0:T(8,128)(2,1)S(1)} %get-tuple-element.14) | copy-start | bytes 393220
  305.3 1.4 copy-start.1
  319.8 0.9 copy-start.4
  319.8 1.0 copy-start.5
  319.8 149.9 %reduce-scatter.8.cloned.1.call-start = ((), (), s32[]{:S(2)}) async-start(), calls=%async_computation.5 | async-start | bytes 3145728 | tf_op jit(solution)/shard_map/reduce_scatter | solution.py:154
  323.3 7.8 %collective-permute-start.2 = (bf16[2,256,128]{1,2,0:T(8,128)(2,1)S(1)}, bf16[2,256,128]{1,2,0:T(8,128)(2,1)S(1)}, u32[]{:S(2)}, u32[]{:S(2)}) collective-permute-start(bf16[2,256,128]{1,2,0:T(8,128)(2,1)S(1)} %get-tuple-element.28), channel_id=1, source_target_pairs={{0,4},{2,6},{4,0},{6,2},{8,12},{10,14},{12,8},{14,10},{16,20},{18,... | collective-permute-start | bytes 393224 | tf_op jit(solution)/shard_map/ppermute | solution.py:13
  331.2 11.1 %collective-permute-start.3 = (bf16[2,256,64]{1,2,0:T(8,128)(2,1)S(1)}, bf16[2,256,64]{1,2,0:T(8,128)(2,1)S(1)}, u32[]{:S(2)}, u32[]{:S(2)}) collective-permute-start(bf16[2,256,64]{1,2,0:T(8,128)(2,1)S(1)} %select_convert_fusion.1), channel_id=1, source_target_pairs={{0,2},{2,0},{4,6},{6,4},{8,10},{10,8},{12,14},{14,12},{16,18},{18,... | collective-permute-start | bytes 196616 | tf_op jit(solution)/shard_map/ppermute | solution.py:13
  348.6 12.0 %copy-start = (bf16[1,2,8192,64]{2,3,1,0:T(8,128)(2,1)S(1)}, bf16[1,2,8192,64]{2,3,1,0:T(8,128)(2,1)}, u32[]{:S(2)}) copy-start(bf16[1,2,8192,64]{2,3,1,0:T(8,128)(2,1)} %all-gather.9.cloned.1.call-done) | copy-start | bytes 6291460
  348.6 245.9 %reduce-scatter.4.cloned.1.call-start = ((), (), s32[]{:S(2)}) async-start(), calls=%async_computation.3 | async-start | bytes 8912896 | tf_op jit(solution)/shard_map/reduce_scatter | solution.py:126
  372.3 171.3 %copy-start.2 = (f32[2,256,256]{1,2,0:T(8,128)S(1)}, f32[2,256,256]{1,2,0:T(8,128)}, u32[]{:S(2)}) copy-start(f32[2,256,256]{1,2,0:T(8,128)} %copy-done.1) | copy-start | bytes 1572868
  431.7 4.6 collective-permute-start.4
  436.2 47.2 %collective-permute-start.5 = (bf16[4096,256]{0,1:T(8,128)(2,1)}, bf16[4096,256]{0,1:T(8,128)(2,1)}, u32[]{:S(2)}, u32[]{:S(2)}) collective-permute-start(bf16[4096,256]{0,1:T(8,128)(2,1)} %collective-permute-done.4), channel_id=1, source_target_pairs={{0,64},{32,96},{64,0},{96,32},{128,192},{160,224},{192,128},{224,1... | collective-permute-start | bytes 6291464 | tf_op jit(solution)/shard_map/ppermute | solution.py:13
  470.8 13.7 %collective-permute-start.7 = (bf16[4096,64]{0,1:T(8,128)(2,1)S(1)}, bf16[4096,64]{0,1:T(8,128)(2,1)S(1)}, u32[]{:S(2)}, u32[]{:S(2)}) collective-permute-start(bf16[4096,64]{0,1:T(8,128)(2,1)S(1)} %slice_bitcast_fusion.2), channel_id=1, source_target_pairs={{0,32},{32,0},{64,96},{96,64},{128,160},{160,128},{192,224},{224,1... | collective-permute-start | bytes 1572872 | tf_op jit(solution)/shard_map/ppermute | solution.py:13
  483.4 72.6 %collective-permute-start.6 = (bf16[4096,256]{0,1:T(8,128)(2,1)}, bf16[4096,256]{0,1:T(8,128)(2,1)}, u32[]{:S(2)}, u32[]{:S(2)}) collective-permute-start(bf16[4096,256]{0,1:T(8,128)(2,1)} %collective-permute-done.5), channel_id=1, source_target_pairs={{0,128},{32,160},{64,192},{96,224},{128,0},{160,32},{192,64},{224,... | collective-permute-start | bytes 6291464 | tf_op jit(solution)/shard_map/ppermute | solution.py:13
  484.6 55.7 %collective-permute-start.8 = (bf16[4096,64]{0,1:T(8,128)(2,1)S(1)}, bf16[4096,64]{0,1:T(8,128)(2,1)S(1)}, u32[]{:S(2)}, u32[]{:S(2)}) collective-permute-start(bf16[4096,64]{0,1:T(8,128)(2,1)S(1)} %collective-permute-done.7), channel_id=1, source_target_pairs={{0,64},{32,96},{64,0},{96,32},{128,192},{160,224},{192,128},{224,1... | collective-permute-start | bytes 1572872 | tf_op jit(solution)/shard_map/ppermute | solution.py:13
  540.2 13.7 %collective-permute-start.9 = (bf16[4096,64]{0,1:T(8,128)(2,1)S(1)}, bf16[4096,64]{0,1:T(8,128)(2,1)S(1)}, u32[]{:S(2)}, u32[]{:S(2)}) collective-permute-start(bf16[4096,64]{0,1:T(8,128)(2,1)S(1)} %collective-permute-done.8), channel_id=1, source_target_pairs={{0,128},{32,160},{64,192},{96,224},{128,0},{160,32},{192,64},{224,... | collective-permute-start | bytes 1572872 | tf_op jit(solution)/shard_map/ppermute | solution.py:13
Sparse Core Ops, SparseCore 0:
  9.8 40.8 all-gather.8
  53.2 124.7 all-gather.6
  180.3 107.8 all-gather.10
  319.9 109.9 reduce-scatter.5
  433.0 36.6 reduce-scatter.7
  473.9 120.5 reduce-scatter.3
where the time goes:
time: 602 us; the launch traced here: 601 us
  waiting for transfers between devices  473 us (79%)
  matrix products  61.1 us (10%)
  starting transfers between devices  26.5 us (4%)
  local copies, waits for them, and re-layouts  17.3 us (3%)
  between operations  14.4 us (2%)
  other arithmetic  9.05 us (2%)
    all_gather x1, waiting for transfers between devices, body(): input_rows = lax.all_gather(hidden[0], 'tensor', axis=2, tiled=True)  127 us
    all_gather x1, waiting for transfers between devices, body(): lax.all_gather(query_weight[0], 'dp', axis=1, tiled=True)  102 us
    ppermute x10, waiting for transfers between devices, from_partner(): return lax.ppermute(value, axis, pairs)  89.3 us
    reduce_scatter x1, waiting for transfers between devices, body(): lax.psum_scatter(query_parts.astype(jnp.float32).astype(jnp.bfloat16), 'd...  57.7 us
    all_gather x1, waiting for transfers between devices, body(): lax.all_gather(keyval_weight[0], 'dp', axis=1, tiled=True)  34.7 us
    reduce_scatter x1, waiting for transfers between devices, body(): lax.psum_scatter(keyval_parts.astype(jnp.float32).astype(jnp.bfloat16), '...  32.9 us
    reduce_scatter x1, waiting for transfers between devices, body(): lax.psum_scatter((row_term + jnp.einsum('hpi,hgi->ghp', keyvalue_gradient...  28 us
    ppermute x10, starting transfers between devices, from_partner(): return lax.ppermute(value, axis, pairs)  26.1 us
  transfers between devices with their start and end apart: 16, of which 13 were waited for; matrix products, arithmetic and copies ran while one was open for 12% of the time, Pallas kernels for 0%

commit v1 on v0

v1 whole, which is shorter than its diff:
```python
import jax
import jax.numpy as jnp
import numpy as np
from jax import lax
from jax.experimental import pallas as pl
from jax.experimental.pallas import tpu as pltpu
from jax.sharding import PartitionSpec as P

MESH = pl.DeviceIdType.MESH
HEAD = 128
TOK = 256
FEAT = 512
F32 = jnp.float32
BF16 = jnp.bfloat16
FLOWS = ((0, 256, "z"),)


def dot(a, b, ca, cb):
    return lax.dot_general(a, b, (((ca,), (cb,)), ((), ())), preferred_element_type=F32)


def pack(v):
    return jnp.concatenate([v[: TOK // 2], v[TOK // 2 :]], axis=1)


def unpack(v):
    v = v.astype(F32)
    return jnp.concatenate([v[:, :64], v[:, 64:]], axis=0)


def kernel(
    hid, wq, wkv, doc, cot, cosf, sinf,
    att_out, hg_out, gq_out, gkv_out,
    X, Wq, Wkv, C, docs, Pq, Pkv, sPq, sPkv, rPq, rPkv, KV, gfp, gsb, grb, Gq, Gkvp, Gkv, Qb, Kb, Vb, att,
    sd, sp, sm, rd, rp, rm, zsd, zsp, zsm, zrd, zrp, zrm, fin, wgq, wgkv,
    ss, rr, ra, ls,
):
    pipe, tens, zl = lax.axis_index("pipe"), lax.axis_index("tensor"), lax.axis_index("dp")
    x, zh = lax.div(tens, 4), lax.rem(tens, 4)
    y, c = lax.div(pipe, 2), lax.rem(pipe, 2)
    own = lax.div(x, 2) == zl

    def dev(x, y, zh, zl, c):
        return {"pipe": y * 2 + c, "tensor": x * 4 + zh, "dp": zl}

    def up(v, k):
        return lax.rem(v + k + 4, 4)

    zflip = 1 - zl
    neighbour = {
        ("x", 1): dev(up(x, 1), y, zh, zl, c),
        ("x", -1): dev(up(x, -1), y, zh, zl, c),
        ("z", 1): dev(x, y, up(zh, 1), zl, c),
        ("z", -1): dev(x, y, up(zh, -1), zl, c),
        ("z", 2): dev(x, y, up(zh, 2), zl, c),
    }
    partner = dev(x, y, zh, zflip, c)
    mirror = dev(x, 3 - y, zh, zl, 1 - c)
    swap0 = dev(3 - x, y, zh, zflip, c)
    swap1 = dev(jnp.where(own, x, 3 - x), 3 - y, zh, jnp.where(own, zl, zflip), 1 - c)

    count = {"s": 0, "r": 0, "l": 0}
    pending = []

    def take(kind):
        count[kind] += 1
        return count[kind] - 1

    def send(src, dst, rsem, to):
        copy = pltpu.make_async_remote_copy(
            src_ref=src, dst_ref=dst, send_sem=ss.at[take("s")], recv_sem=rsem, device_id=to, device_id_type=MESH
        )
        copy.start()
        pending.append(copy)

    def arrived(dst, rsem, frm):
        pltpu.make_async_remote_copy(
            src_ref=dst, dst_ref=dst, send_sem=ss.at[0], recv_sem=rsem, device_id=frm, device_id_type=MESH
        ).wait_recv()

    def local(src, dst):
        copy = pltpu.make_async_copy(src, dst, ls.at[take("l")])
        copy.start()
        return copy

    load_wq = local(wq.at[0], Wq)
    load_wkv = local(wkv.at[0], Wkv)
    load_c = local(cot.at[0], C.at[0])

    barrier = pltpu.get_barrier_semaphore()
    greet0 = dev(
        jnp.where(own, x, 3 - x), jnp.where(own, 3 - y, y), zh, jnp.where(own, zl, zflip), jnp.where(own, 1 - c, c)
    )
    for to in list(neighbour.values()) + [partner, mirror, swap1, greet0]:
        pl.semaphore_signal(barrier, inc=1, device_id=to, device_id_type=MESH)
    pl.semaphore_wait(barrier, 9)

    s1r = rr.at[take("r")]
    send(hid.at[1], X.at[1, jnp.where(own, x, 3 - x), zh], s1r, swap1)
    s0s, s0r, s0l = ss.at[take("s")], rr.at[take("r")], ls.at[take("l")]

    @pl.when(own)
    def _():
        copy = pltpu.make_async_copy(hid.at[0], X.at[0, x, zh], s0l)
        copy.start()
        copy.wait()

    @pl.when(jnp.logical_not(own))
    def _():
        copy = pltpu.make_async_remote_copy(
            src_ref=hid.at[0], dst_ref=X.at[0, 3 - x, zh], send_sem=s0s, recv_sem=s0r, device_id=swap0, device_id_type=MESH
        )
        copy.start()
        copy.wait()

    Pq[...] = jnp.zeros_like(Pq)
    Pkv[...] = jnp.zeros_like(Pkv)

    cr, dr = rr.at[take("r")], rr.at[take("r")]

    def send_small():
        send(cot.at[1], C.at[1], cr, mirror)
        send(doc.at[1], docs, dr, mirror)

    def block(xs, zs):
        bit = lax.rem(lax.rem(xs, 2) + lax.div(xs, 2) + zl, 2)
        return pl.multiple_of((bit * 4 + zs) * FEAT, FEAT)

    def project(e, xs, zs):
        d = lax.div(xs, 2)
        rows = pl.ds(block(xs, zs), FEAT)
        xb = X[e, xs, zs]
        Pq[e, d] += dot(xb, Wq[rows, :], 1, 0)
        Pkv[e, d] += dot(xb, Wkv[rows, :], 1, 0)

    pos = {"x": x, "z": zh}

    def slot(first, a, b):
        return (a, b) if first == "x" else (b, a)

    def part(flow, half):
        r0, n, _ = FLOWS[flow]
        if half is None:
            return pl.ds(r0, n)
        return pl.ds(r0 + half * (n // 2), n // 2)

    def fwd(f, e, s, half, axis, sign):
        ref = X.at[e, s[0], s[1], part(f, half)]
        send(ref, ref, ra.at[f, e, s[0], s[1], half or 0], neighbour[(axis, sign)])

    def got(f, e, s, half, axis, sign):
        ref = X.at[e, s[0], s[1], part(f, half)]
        arrived(ref, ra.at[f, e, s[0], s[1], half or 0], neighbour[(axis, sign)])

    def axes(f):
        first = FLOWS[f][2]
        second = "z" if first == "x" else "x"
        return first, second, pos[first], pos[second]

    flows = range(len(FLOWS))

    def gather_first(e):
        for f in flows:
            A, B, a, b = axes(f)
            s = slot(A, a, b)
            fwd(f, e, s, None, A, 1)
            fwd(f, e, s, None, A, -1)
            fwd(f, e, s, None, B, 1)
            fwd(f, e, s, None, B, -1)

    def gather_second(e):
        for f in flows:
            A, B, a, b = axes(f)
            s = slot(A, up(a, -1), b)
            got(f, e, s, None, A, -1)
            fwd(f, e, s, 0, A, 1)
            fwd(f, e, s, None, B, 1)
            fwd(f, e, s, None, B, -1)
            s = slot(A, up(a, 1), b)
            got(f, e, s, None, A, 1)
            fwd(f, e, s, 1, A, -1)
            fwd(f, e, s, None, B, 1)
            fwd(f, e, s, None, B, -1)

    def gather_third(e):
        for f in flows:
            A, B, a, b = axes(f)
            s = slot(A, up(a, 2), b)
            got(f, e, s, 0, A, -1)
            got(f, e, s, 1, A, 1)
            fwd(f, e, s, None, B, 1)
            fwd(f, e, s, None, B, -1)

    def gather_near(e, k):
        for f in flows:
            A, B, a, b = axes(f)
            s = slot(A, up(a, k), up(b, -1))
            got(f, e, s, None, B, -1)
            fwd(f, e, s, 0, B, 1)
            s = slot(A, up(a, k), up(b, 1))
            got(f, e, s, None, B, 1)
            fwd(f, e, s, 1, B, -1)

    def gather_far(e, k):
        for f in flows:
            A, B, a, b = axes(f)
            s = slot(A, up(a, k), up(b, 2))
            got(f, e, s, 0, B, -1)
            got(f, e, s, 1, B, 1)

    ORDER = (0, -1, 1, 2)

    gather_first(0)
    arrived(X.at[1, x, zh], s1r, swap1)
    gather_first(1)
    send_small()
    load_wq.wait()
    load_wkv.wait()
    for e in (0, 1):
        project(e, x, zh)
    for e in (0, 1):
        gather_second(e)
    for e in (0, 1):
        if len(FLOWS) == 1:
            project(e, x, up(zh, -1))
            project(e, x, up(zh, 1))
    for e in (0, 1):
        gather_third(e)
    for e in (0, 1):
        if len(FLOWS) == 1:
            project(e, x, up(zh, 2))
    for k in ORDER:
        for e in (0, 1):
            gather_near(e, k)
            if len(FLOWS) == 1:
                project(e, up(x, -1), up(zh, k))
                project(e, up(x, 1), up(zh, k))
    for k in ORDER:
        for e in (0, 1):
            gather_far(e, k)
            if len(FLOWS) == 1:
                project(e, up(x, 2), up(zh, k))
    if len(FLOWS) > 1:
        for e in (0, 1):
            for i in ORDER:
                for k in ORDER:
                    if (i, k) != (0, 0):
                        project(e, up(x, i), up(zh, k))

    pr = [(rr.at[take("r")], rr.at[take("r")]) for e in (0, 1)]
    for e in (0, 1):
        sPq[e] = Pq[e, zflip].astype(BF16)
        send(sPq.at[e], rPq.at[e], pr[e][0], partner)
        sPkv[e] = pack(Pkv[e, zflip]).astype(BF16)
        send(sPkv.at[e], rPkv.at[e], pr[e][1], partner)

    kvr = [[rr.at[take("r")] for o in (1, 2, 3)] for e in (0, 1)]
    zto = {1: neighbour[("z", 1)], 2: neighbour[("z", 2)], 3: neighbour[("z", -1)]}
    zfrom = {1: neighbour[("z", -1)], 2: neighbour[("z", 2)], 3: neighbour[("z", 1)]}
    for e in (0, 1):
        arrived(rPkv.at[e], pr[e][1], partner)
        piece = pack(Pkv[e, zl]) + rPkv[e].astype(F32)
        KV[e, zh] = piece.astype(BF16)
        for o in (1, 2, 3):
            send(KV.at[e, zh], KV.at[e, zh], kvr[e][o - 1], zto[o])

    cosw, sinw = cosf[...], sinf[...]

    def rope(v):
        return v * cosw + pltpu.roll(v, 64, 1) * sinw

    def unrope(v):
        return v * cosw - pltpu.roll(v, 64, 1) * sinw

    for e in (0, 1):
        arrived(rPq.at[e], pr[e][0], partner)
        q = Pq[e, zl] + rPq[e].astype(F32)
        Qb[e, 0] = rope(q[:, :HEAD]).astype(BF16)
        Qb[e, 1] = rope(q[:, HEAD:]).astype(BF16)

    load_c.wait()
    arrived(C.at[1], cr, mirror)
    arrived(docs, dr, mirror)
    scale = HEAD**-0.5
    ar = [rr.at[take("r")] for _ in (0,)]
    gr = [[rr.at[take("r")] for o in (1, 2, 3)] for e in (0, 1)]
    row = lax.broadcasted_iota(jnp.int32, (TOK, TOK), 0)
    col = lax.broadcasted_iota(jnp.int32, (TOK, TOK), 1)
    for e in (0, 1):
        for o in (1, 2, 3):
            frm = up(zh, -o)
            arrived(KV.at[e, frm], kvr[e][o - 1], zfrom[o])
        kraw = jnp.concatenate([unpack(KV[e, 0]), unpack(KV[e, 1])], axis=1)
        keys = rope(kraw).astype(BF16)
        values = jnp.concatenate([unpack(KV[e, 2]), unpack(KV[e, 3])], axis=1).astype(BF16)
        ids = doc[0] if e == 0 else docs[...]
        wide = jnp.broadcast_to(ids.astype(F32), (TOK, TOK))
        allowed = (wide == wide.T) & (col <= row)
        gk = jnp.zeros((TOK, HEAD), F32)
        gv = jnp.zeros((TOK, HEAD), F32)
        for j in (0, 1):
            q = Qb[e, j]
            g = C[e, :, j * HEAD : (j + 1) * HEAD]
            weights = jnp.where(allowed, jnp.exp(dot(q, keys, 1, 1) * scale), 0.0)
            probs = weights / jnp.sum(weights, axis=-1, keepdims=True)
            low = probs.astype(BF16)
            att[e, :, j * HEAD : (j + 1) * HEAD] = dot(low, values, 1, 0).astype(BF16)
            gv = gv + dot(low, g, 0, 0)
            gp = dot(g, values, 1, 1)
            rdot = jnp.sum(gp * probs, axis=-1, keepdims=True)
            gs = (probs * (gp - rdot) * scale).astype(BF16)
            Gq[e, zl, :, j * HEAD : (j + 1) * HEAD] = unrope(dot(gs, keys, 1, 0)).astype(BF16)
            gk = gk + dot(gs, q, 0, 0)
        gk = unrope(gk)
        for i, v in enumerate((gk[:, :64], gk[:, 64:], gv[:, :64], gv[:, 64:])):
            v = pack(v)
            gfp[e, i] = v
            gsb[e, i] = v.astype(BF16)
        for o in (1, 2, 3):
            send(gsb.at[e, up(zh, o)], grb.at[e, o - 1], gr[e][o - 1], zto[o])
    save_att = local(att.at[0], att_out.at[0])
    send(att.at[1], att_out.at[1], ar[0], mirror)

    xr = [(rr.at[take("r")], rr.at[take("r")]) for e in (0, 1)]
    for e in (0, 1):
        send(Gq.at[e, zl], Gq.at[e, zl], xr[e][0], partner)
    for e in (0, 1):
        total = gfp[e, zh]
        for o in (1, 2, 3):
            arrived(grb.at[e, o - 1], gr[e][o - 1], zfrom[o])
            total = total + grb[e, o - 1].astype(F32)
        Gkvp[e, zl] = total.astype(BF16)
        send(Gkvp.at[e, zl], Gkvp.at[e, zl], xr[e][1], partner)
    for e in (0, 1):
        arrived(Gq.at[e, zflip], xr[e][0], partner)
        arrived(Gkvp.at[e, zflip], xr[e][1], partner)
        for d in (0, 1):
            Gkv[e, d] = unpack(Gkvp[e, d]).astype(BF16)

    def term(f, e, s):
        xs, zs = s
        d = lax.div(xs, 2)
        rows = pl.ds(block(xs, zs), FEAT)
        return dot(Gq[e, d, part(f, None)], Wq[rows, :], 1, 1) + dot(Gkv[e, d, part(f, None)], Wkv[rows, :], 1, 1)

    BACK = (2, 1, -1, 0)
    sem = {}

    def rsem(*key):
        if key not in sem:
            sem[key] = rr.at[take("r")]
        return sem[key]

    def raxes(f):
        B, A, b, a = axes(f)
        return A, B, a, b

    def rslot(f, a, b):
        A, B, _, _ = raxes(f)
        return slot(A, a, b)

    def scatter_far(e, i):
        k = BACK[i]
        for f in flows:
            A, B, a, b = raxes(f)
            sd[e, i, part(f, None)] = term(f, e, rslot(f, up(a, 2), up(b, k))).astype(BF16)
            for half, sign in ((0, 1), (1, -1)):
                send(sd.at[e, i, part(f, half)], rd.at[e, i, part(f, half)], rsem("d", f, e, i, half), neighbour[(A, sign)])

    def add_half(f, v, ref, half):
        n = FLOWS[f][1] // 2
        other = ref.astype(F32)
        if half == 0:
            return jnp.concatenate([v[:n] + other, v[n:]], axis=0)
        return jnp.concatenate([v[:n], v[n:] + other], axis=0)

    def scatter_near(e, i):
        k = BACK[i]
        for f in flows:
            A, B, a, b = raxes(f)
            for half, sign, out, into in ((0, 1, sp, rp), (1, -1, sm, rm)):
                v = term(f, e, rslot(f, up(a, sign), up(b, k)))
                arrived(rd.at[e, i, part(f, half)], rsem("d", f, e, i, half), neighbour[(A, -sign)])
                v = add_half(f, v, rd[e, i, part(f, half)], half)
                out[e, i, part(f, None)] = v.astype(BF16)
                send(out.at[e, i, part(f, None)], into.at[e, i, part(f, None)], rsem("n", f, e, i, half), neighbour[(A, sign)])

    def scatter_own(e, i):
        k = BACK[i]
        for f in flows:
            A, B, a, b = raxes(f)
            rows = part(f, None)
            v = term(f, e, rslot(f, a, up(b, k)))
            for half, sign, into in ((0, 1, rp), (1, -1, rm)):
                arrived(into.at[e, i, rows], rsem("n", f, e, i, half), neighbour[(A, -sign)])
                v = v + into[e, i, rows].astype(F32)
            if k == 2:
                zsd[e, rows] = v.astype(BF16)
                for half, sign in ((0, 1), (1, -1)):
                    send(zsd.at[e, part(f, half)], zrd.at[e, part(f, half)], rsem("zd", f, e, half), neighbour[(B, sign)])
            elif k in (1, -1):
                half, out, into = (0, zsp, zrp) if k == 1 else (1, zsm, zrm)
                arrived(zrd.at[e, part(f, half)], rsem("zd", f, e, half), neighbour[(B, -k)])
                v = add_half(f, v, zrd[e, part(f, half)], half)
                out[e, rows] = v.astype(BF16)
                send(out.at[e, rows], into.at[e, rows], rsem("zn", f, e, half), neighbour[(B, k)])
            else:
                for half, sign, into in ((0, 1, zrp), (1, -1, zrm)):
                    arrived(into.at[e, rows], rsem("zn", f, e, half), neighbour[(B, -sign)])
                    v = v + into[e, rows].astype(F32)
                fin[e, rows] = v.astype(BF16)

    save = []

    def weight_grads(i):
        bit, zs = i // 4, i % 4
        tq = jnp.zeros((FEAT, TOK), F32)
        tkv = jnp.zeros((FEAT, 64), F32)
        for d in (0, 1):
            xs = 2 * d + lax.rem(bit + d + zl, 2)
            for e in (0, 1):
                xb = X[e, xs, zs]
                tq = tq + dot(xb, Gq[e, d], 0, 0)
                tkv = tkv + dot(xb, Gkv[e, d], 0, 0)
        wgq[i] = tq
        wgkv[i] = tkv
        save.append(local(wgq.at[i], gq_out.at[pl.ds(i * FEAT, FEAT)]))
        save.append(local(wgkv.at[i], gkv_out.at[pl.ds(i * FEAT, FEAT)]))

    for i in range(4):
        for e in (0, 1):
            scatter_far(e, i)
    for i in range(4):
        for e in (0, 1):
            scatter_near(e, i)
        weight_grads(i)
    for i in range(4):
        weight_grads(4 + i)
        for e in (0, 1):
            scatter_own(e, i)

    f1r = rr.at[take("r")]
    send(fin.at[1], hg_out.at[1], f1r, swap1)
    f0s, f0r, f0l = ss.at[take("s")], rr.at[take("r")], ls.at[take("l")]

    @pl.when(own)
    def _():
        copy = pltpu.make_async_copy(fin.at[0], hg_out.at[0], f0l)
        copy.start()
        copy.wait()

    @pl.when(jnp.logical_not(own))
    def _():
        copy = pltpu.make_async_remote_copy(
            src_ref=fin.at[0], dst_ref=hg_out.at[0], send_sem=f0s, recv_sem=f0r, device_id=swap0, device_id_type=MESH
        )
        copy.start()
        copy.wait()

    arrived(hg_out.at[1], f1r, swap1)
    arrived(att_out.at[1], ar[0], mirror)
    save_att.wait()
    for copy in save:
        copy.wait()
    for copy in pending:
        copy.wait_send()


def rope_tables():
    freqs = 10000.0 ** (-2.0 * np.arange(HEAD // 2) / HEAD)
    angles = np.arange(TOK, dtype=np.float32)[:, None] * freqs.astype(np.float32)[None, :]
    cosine, sine = np.cos(angles), np.sin(angles)
    return (
        np.concatenate([cosine, cosine], 1).astype(np.float32),
        np.concatenate([-sine, sine], 1).astype(np.float32),
    )


def body(hidden, query_weight, keyval_weight, doc_ids, cotangent):
    cosf, sinf = rope_tables()
    anywhere = pl.BlockSpec(memory_space=pl.ANY)
    vmem = pl.BlockSpec(memory_space=pltpu.VMEM)
    V = pltpu.VMEM
    big = V((2, 4, TOK, FEAT), BF16)
    mid = V((2, TOK, FEAT), BF16)
    nf = len(FLOWS)
    scratch = [
        V((2, 4, 4, TOK, FEAT), BF16),
        V((4096, 256), BF16), V((4096, 64), BF16),
        V((2, TOK, 256), BF16), V((1, TOK), jnp.int32),
        V((2, 2, TOK, 256), F32), V((2, 2, TOK, 64), F32),
        V((2, TOK, 256), BF16), V((2, 128, 128), BF16), V((2, TOK, 256), BF16), V((2, 128, 128), BF16),
        V((2, 4, 128, 128), BF16),
        V((2, 4, 128, 128), F32), V((2, 4, 128, 128), BF16), V((2, 3, 128, 128), BF16),
        V((2, 2, TOK, 256), BF16), V((2, 2, 128, 128), BF16), V((2, 2, TOK, 64), BF16),
        V((2, 2, TOK, HEAD), BF16), V((2, TOK, HEAD), BF16), V((2, TOK, HEAD), BF16),
        V((2, TOK, 256), BF16),
        big, big, big, big, big, big,
        mid, mid, mid, mid, mid, mid, mid,
        V((8, FEAT, 256), F32), V((8, FEAT, 64), F32),
        pltpu.SemaphoreType.DMA((64 + 96 * nf,)),
        pltpu.SemaphoreType.DMA((48 + 48 * nf,)),
        pltpu.SemaphoreType.DMA((nf, 2, 4, 4, 2)),
        pltpu.SemaphoreType.DMA((32,)),
    ]
    att, hg, gq, gkv = pl.pallas_call(
        kernel,
        out_shape=(
            jax.ShapeDtypeStruct((2, TOK, 256), BF16),
            jax.ShapeDtypeStruct((2, TOK, FEAT), BF16),
            jax.ShapeDtypeStruct((4096, 256), F32),
            jax.ShapeDtypeStruct((4096, 64), F32),
        ),
        in_specs=[anywhere, anywhere, anywhere, vmem, anywhere, vmem, vmem],
        out_specs=(anywhere,) * 4,
        scratch_shapes=scratch,
        compiler_params=pltpu.CompilerParams(
            collective_id=0, has_side_effects=True, vmem_limit_bytes=60 * 2**20
        ),
    )(hidden[0], query_weight[0], keyval_weight[0], doc_ids[0], cotangent[0], cosf, sinf)
    return att[None], hg[None], gq[None], gkv[None]


def solution(mesh):
    sharded = P("pipe", None, "dp", "tensor")
    return jax.shard_map(
        body,
        mesh=mesh,
        in_specs=(sharded, sharded, sharded, P("pipe", None, "dp", None), sharded),
        out_specs=(sharded, sharded, P("pipe", "dp", "tensor"), P("pipe", "dp", "tensor")),
        check_vma=False,
    )
```

time: 602 us -> 250 us (0.42)
  waiting for transfers between devices: 473 us -> 0 us
  Pallas kernels: 0 us -> 232 us
  matrix products: 61.1 us -> 0 us
  starting transfers between devices: 26.5 us -> 0 us
  between operations: 14.4 us -> 0.64 us
  other arithmetic: 9.05 us -> 0 us
    all_gather x3 -> x0, waiting for transfers between devices: 264 us -> none  [the longest x1 127 us: body(): input_rows = lax.all_gather(hidden[0], 'tensor', axis=2, tiled=True)]
    pallas_call x0 -> x1, Pallas kernels: none -> 232 us  [body(): pl.pallas_call(kernel, out_shape=(jax.ShapeDtypeStruct((2, TOK, 256), BF1...]
    reduce_scatter x3 -> x0, waiting for transfers between devices: 119 us -> none  [the longest x1 57.7 us: body(): lax.psum_scatter(query_parts.astype(jnp.float32).astype(jnp.bfloat16), 'd...]
    ppermute x10 -> x0, waiting for transfers between devices: 89.3 us -> none  [from_partner(): return lax.ppermute(value, axis, pairs)]
    dot_general x11 -> x0, matrix products: 59.6 us -> none  [the longest x1 11.9 us: body(): jnp.einsum('hpi,hgi->ghp', query_gradient, query_pieces, preferred_elemen...]
    ppermute x10 -> x0, starting transfers between devices: 26.1 us -> none  [from_partner(): return lax.ppermute(value, axis, pairs)]
    broadcast_in_dim x2 -> x0, other arithmetic: 7.04 us -> none  [the longest x1 4.92 us: body(): query_grad[None]]
    unnamed x22 -> x5, local copies, waits for them, and re-layouts: 14 us -> 13.9 us
  transfers between devices with their start and end apart: 16 -> 0, of which waited for: 13 -> 0; matrix products, arithmetic and copies ran while one was open for 12% -> 0% of each run, Pallas kernels for 0% -> 0%
where the time goes in v1:
time: 250 us; the launch traced here: 246 us
  Pallas kernels  232 us (93%)
  local copies, waits for them, and re-layouts  13.9 us (6%)
    pallas_call x1, Pallas kernels, body(): pl.pallas_call(kernel, out_shape=(jax.ShapeDtypeStruct((2, TOK, 256), BF1...  232 us
    unnamed x5, local copies, waits for them, and re-layouts  13.9 us

profile of v1, /device:TPU:31, one launch (start us, length us, event | category | flops | bytes accessed | tf_op | source)
XLA Modules:
  0.0 246.3 jit_solution(4707579974292860863)
XLA Ops:
  0.6 2.7 %copy.11 = bf16[1,2,4096,64]{3,2,1,0:T(8,128)(2,1)} copy(bf16[1,2,4096,64]{2,3,1,0:T(8,128)(2,1)} %param.9) | data formatting | bytes 2097152 | tf_op args[2]
  3.3 231.7 %shard_map.102 = (bf16[2,256,256]{2,1,0:T(8,128)(2,1)}, bf16[2,256,512]{2,1,0:T(8,128)(2,1)}, f32[4096,256]{1,0:T(8,128)}, f32[4096,64]{1,0:T(8,128)}) custom-call(bf16[2,256,512]{2,1,0:T(8,128)(2,1)} %bitcast.14, bf16[2,4096,256]{2,1,0:T(8,128)(2,1)} %bitcast.10, bf16[2,4096,64]{2,1,0:T(8,128)(2,1)} %bitcast.9, s32[2,1,256]{2,1,0:T(1,128)} %bitcast.17, ...), custom_call_target="tpu_custom_call" | custom-call | tf_op jit(solution)/shard_map/pallas_call | solution.py:506
  235.1 3.1 %copy.12 = f32[1,4096,64]{1,2,0:T(8,128)} copy(f32[1,4096,64]{2,1,0:T(8,128)} %bitcast.12) | data formatting | bytes 2097152
  238.3 1.7 copy.16
  239.9 1.9 copy.17
  241.8 4.5 %copy.18 = f32[1,4096,256]{2,1,0:T(8,128)} copy(f32[1,4096,256]{2,1,0:T(8,128)} %bitcast.11) | data formatting | bytes 8388608

commit v2 on v1

--- a/solution.py
+++ b/solution.py
@@ -12,7 +12,7 @@
 FEAT = 512
 F32 = jnp.float32
 BF16 = jnp.bfloat16
-FLOWS = ((0, 256, "z"),)
+FLOWS = ((0, 192, "z"), (192, 64, "x"))
 
 
 def dot(a, b, ca, cb):
@@ -31,7 +31,7 @@
 def kernel(
     hid, wq, wkv, doc, cot, cosf, sinf,
     att_out, hg_out, gq_out, gkv_out,
-    X, Wq, Wkv, C, docs, Pq, Pkv, sPq, sPkv, rPq, rPkv, KV, gfp, gsb, grb, Gq, Gkvp, Gkv, Qb, Kb, Vb, att,
+    X, Wq, Wkv, C, docs, Pq, Pkv, sPq, sPkv, rPq, rPkv, KV, gfp, gsb, grb, Gq, Gkvp, Gkv, Qb, att,
     sd, sp, sm, rd, rp, rm, zsd, zsp, zsm, zrd, zrp, zrm, fin, wgq, wgkv,
     ss, rr, ra, ls,
 ):
@@ -61,6 +61,7 @@
 
     count = {"s": 0, "r": 0, "l": 0}
     pending = []
+    save = []
 
     def take(kind):
         count[kind] += 1
@@ -82,10 +83,6 @@
         copy = pltpu.make_async_copy(src, dst, ls.at[take("l")])
         copy.start()
         return copy
-
-    load_wq = local(wq.at[0], Wq)
-    load_wkv = local(wkv.at[0], Wkv)
-    load_c = local(cot.at[0], C.at[0])
 
     barrier = pltpu.get_barrier_semaphore()
     greet0 = dev(
@@ -95,32 +92,37 @@
         pl.semaphore_signal(barrier, inc=1, device_id=to, device_id_type=MESH)
     pl.semaphore_wait(barrier, 9)
 
-    s1r = rr.at[take("r")]
+    s0s, s0r, s0l = ss.at[take("s")], rr.at[take("r")], ls.at[take("l")]
+
+    def keep(src, dst, start):
+        copy = pltpu.make_async_copy(src, dst, s0l)
+        copy.start() if start else copy.wait()
+
+    def swap(src, dst, start):
+        copy = pltpu.make_async_remote_copy(
+            src_ref=src, dst_ref=dst, send_sem=s0s, recv_sem=s0r, device_id=swap0, device_id_type=MESH
+        )
+        copy.start() if start else copy.wait()
+
+    def stage0(start):
+        @pl.when(own)
+        def _():
+            keep(hid.at[0], X.at[0, x, zh], start)
+
+        @pl.when(jnp.logical_not(own))
+        def _():
+            swap(hid.at[0], X.at[0, 3 - x, zh], start)
+
+    s1r, cr, dr = rr.at[take("r")], rr.at[take("r")], rr.at[take("r")]
+    stage0(True)
     send(hid.at[1], X.at[1, jnp.where(own, x, 3 - x), zh], s1r, swap1)
-    s0s, s0r, s0l = ss.at[take("s")], rr.at[take("r")], ls.at[take("l")]
-
-    @pl.when(own)
-    def _():
-        copy = pltpu.make_async_copy(hid.at[0], X.at[0, x, zh], s0l)
-        copy.start()
-        copy.wait()
-
-    @pl.when(jnp.logical_not(own))
-    def _():
-        copy = pltpu.make_async_remote_copy(
-            src_ref=hid.at[0], dst_ref=X.at[0, 3 - x, zh], send_sem=s0s, recv_sem=s0r, device_id=swap0, device_id_type=MESH
-        )
-        copy.start()
-        copy.wait()
-
+    load_wq = local(wq.at[0], Wq)
+    load_wkv = local(wkv.at[0], Wkv)
+    load_c = local(cot.at[0], C.at[0])
+    send(cot.at[1], C.at[1], cr, mirror)
+    send(doc.at[1], docs, dr, mirror)
     Pq[...] = jnp.zeros_like(Pq)
     Pkv[...] = jnp.zeros_like(Pkv)
-
-    cr, dr = rr.at[take("r")], rr.at[take("r")]
-
-    def send_small():
-        send(cot.at[1], C.at[1], cr, mirror)
-        send(doc.at[1], docs, dr, mirror)
 
     def block(xs, zs):
         bit = lax.rem(lax.rem(xs, 2) + lax.div(xs, 2) + zl, 2)
@@ -131,7 +133,7 @@
         rows = pl.ds(block(xs, zs), FEAT)
         xb = X[e, xs, zs]
         Pq[e, d] += dot(xb, Wq[rows, :], 1, 0)
-        Pkv[e, d] += dot(xb, Wkv[rows, :], 1, 0)
+        Pkv[e, d] += dot(xb, Wkv[:, rows], 1, 1)
 
     pos = {"x": x, "z": zh}
 
@@ -210,92 +212,67 @@
 
     ORDER = (0, -1, 1, 2)
 
-    gather_first(0)
-    arrived(X.at[1, x, zh], s1r, swap1)
-    gather_first(1)
-    send_small()
-    load_wq.wait()
-    load_wkv.wait()
-    for e in (0, 1):
-        project(e, x, zh)
-    for e in (0, 1):
-        gather_second(e)
-    for e in (0, 1):
-        if len(FLOWS) == 1:
-            project(e, x, up(zh, -1))
-            project(e, x, up(zh, 1))
-    for e in (0, 1):
-        gather_third(e)
-    for e in (0, 1):
-        if len(FLOWS) == 1:
-            project(e, x, up(zh, 2))
-    for k in ORDER:
-        for e in (0, 1):
-            gather_near(e, k)
-            if len(FLOWS) == 1:
-                project(e, up(x, -1), up(zh, k))
-                project(e, up(x, 1), up(zh, k))
-    for k in ORDER:
-        for e in (0, 1):
-            gather_far(e, k)
-            if len(FLOWS) == 1:
-                project(e, up(x, 2), up(zh, k))
-    if len(FLOWS) > 1:
-        for e in (0, 1):
-            for i in ORDER:
-                for k in ORDER:
-                    if (i, k) != (0, 0):
-                        project(e, up(x, i), up(zh, k))
-
+    def project_near(e):
+        for i in (-1, 0, 1):
+            for k in (-1, 0, 1):
+                project(e, up(x, i), up(zh, k))
+
+    def project_far(e):
+        for i in ORDER:
+            for k in ORDER:
+                if i == 2 or k == 2:
+                    project(e, up(x, i), up(zh, k))
+
+    cosw, sinw = cosf[...], sinf[...]
+
+    def rope(v):
+        return v * cosw + pltpu.roll(v, 64, 1) * sinw
+
+    def unrope(v):
+        return v * cosw - pltpu.roll(v, 64, 1) * sinw
+
+    zto = {1: neighbour[("z", 1)], 2: neighbour[("z", 2)], 3: neighbour[("z", -1)]}
+    zfrom = {1: neighbour[("z", -1)], 2: neighbour[("z", 2)], 3: neighbour[("z", 1)]}
     pr = [(rr.at[take("r")], rr.at[take("r")]) for e in (0, 1)]
-    for e in (0, 1):
+    kvr = [[rr.at[take("r")] for o in (1, 2, 3)] for e in (0, 1)]
+    gr = [[rr.at[take("r")] for o in (1, 2, 3)] for e in (0, 1)]
+    xr = [(rr.at[take("r")], rr.at[take("r")]) for e in (0, 1)]
+    ar = rr.at[take("r")]
+    scale = HEAD**-0.5
+
+    def send_partial(e):
+        sPkv[e] = pack(Pkv[e, zflip]).astype(BF16)
+        send(sPkv.at[e], rPkv.at[e], pr[e][1], partner)
         sPq[e] = Pq[e, zflip].astype(BF16)
         send(sPq.at[e], rPq.at[e], pr[e][0], partner)
-        sPkv[e] = pack(Pkv[e, zflip]).astype(BF16)
-        send(sPkv.at[e], rPkv.at[e], pr[e][1], partner)
-
-    kvr = [[rr.at[take("r")] for o in (1, 2, 3)] for e in (0, 1)]
-    zto = {1: neighbour[("z", 1)], 2: neighbour[("z", 2)], 3: neighbour[("z", -1)]}
-    zfrom = {1: neighbour[("z", -1)], 2: neighbour[("z", 2)], 3: neighbour[("z", 1)]}
-    for e in (0, 1):
+
+    def send_kv(e):
         arrived(rPkv.at[e], pr[e][1], partner)
         piece = pack(Pkv[e, zl]) + rPkv[e].astype(F32)
         KV[e, zh] = piece.astype(BF16)
         for o in (1, 2, 3):
             send(KV.at[e, zh], KV.at[e, zh], kvr[e][o - 1], zto[o])
-
-    cosw, sinw = cosf[...], sinf[...]
-
-    def rope(v):
-        return v * cosw + pltpu.roll(v, 64, 1) * sinw
-
-    def unrope(v):
-        return v * cosw - pltpu.roll(v, 64, 1) * sinw
-
-    for e in (0, 1):
         arrived(rPq.at[e], pr[e][0], partner)
         q = Pq[e, zl] + rPq[e].astype(F32)
         Qb[e, 0] = rope(q[:, :HEAD]).astype(BF16)
         Qb[e, 1] = rope(q[:, HEAD:]).astype(BF16)
 
-    load_c.wait()
-    arrived(C.at[1], cr, mirror)
-    arrived(docs, dr, mirror)
-    scale = HEAD**-0.5
-    ar = [rr.at[take("r")] for _ in (0,)]
-    gr = [[rr.at[take("r")] for o in (1, 2, 3)] for e in (0, 1)]
-    row = lax.broadcasted_iota(jnp.int32, (TOK, TOK), 0)
-    col = lax.broadcasted_iota(jnp.int32, (TOK, TOK), 1)
-    for e in (0, 1):
+    def attend(e):
+        if e == 0:
+            load_c.wait()
+        else:
+            arrived(C.at[1], cr, mirror)
+            arrived(docs, dr, mirror)
+        row = lax.broadcasted_iota(jnp.int32, (TOK, TOK), 0)
+        col = lax.broadcasted_iota(jnp.int32, (TOK, TOK), 1)
+        ids = doc[0] if e == 0 else docs[...]
+        wide = jnp.broadcast_to(ids.astype(F32), (TOK, TOK))
+        allowed = (wide == wide.T) & (col <= row)
         for o in (1, 2, 3):
-            frm = up(zh, -o)
-            arrived(KV.at[e, frm], kvr[e][o - 1], zfrom[o])
+            arrived(KV.at[e, up(zh, -o)], kvr[e][o - 1], zfrom[o])
         kraw = jnp.concatenate([unpack(KV[e, 0]), unpack(KV[e, 1])], axis=1)
         keys = rope(kraw).astype(BF16)
         values = jnp.concatenate([unpack(KV[e, 2]), unpack(KV[e, 3])], axis=1).astype(BF16)
-        ids = doc[0] if e == 0 else docs[...]
-        wide = jnp.broadcast_to(ids.astype(F32), (TOK, TOK))
-        allowed = (wide == wide.T) & (col <= row)
         gk = jnp.zeros((TOK, HEAD), F32)
         gv = jnp.zeros((TOK, HEAD), F32)
         for j in (0, 1):
@@ -318,20 +295,21 @@
             gsb[e, i] = v.astype(BF16)
         for o in (1, 2, 3):
             send(gsb.at[e, up(zh, o)], grb.at[e, o - 1], gr[e][o - 1], zto[o])
-    save_att = local(att.at[0], att_out.at[0])
-    send(att.at[1], att_out.at[1], ar[0], mirror)
-
-    xr = [(rr.at[take("r")], rr.at[take("r")]) for e in (0, 1)]
-    for e in (0, 1):
         send(Gq.at[e, zl], Gq.at[e, zl], xr[e][0], partner)
-    for e in (0, 1):
+        if e == 0:
+            save.append(local(att.at[0], att_out.at[0]))
+        else:
+            send(att.at[1], att_out.at[1], ar, mirror)
+
+    def send_gkv(e):
         total = gfp[e, zh]
         for o in (1, 2, 3):
             arrived(grb.at[e, o - 1], gr[e][o - 1], zfrom[o])
             total = total + grb[e, o - 1].astype(F32)
         Gkvp[e, zl] = total.astype(BF16)
         send(Gkvp.at[e, zl], Gkvp.at[e, zl], xr[e][1], partner)
-    for e in (0, 1):
+
+    def take_g(e):
         arrived(Gq.at[e, zflip], xr[e][0], partner)
         arrived(Gkvp.at[e, zflip], xr[e][1], partner)
         for d in (0, 1):
@@ -341,7 +319,7 @@
         xs, zs = s
         d = lax.div(xs, 2)
         rows = pl.ds(block(xs, zs), FEAT)
-        return dot(Gq[e, d, part(f, None)], Wq[rows, :], 1, 1) + dot(Gkv[e, d, part(f, None)], Wkv[rows, :], 1, 1)
+        return dot(Gq[e, d, part(f, None)], Wq[rows, :], 1, 1) + dot(Gkv[e, d, part(f, None)], Wkv[:, rows], 1, 0)
 
     BACK = (2, 1, -1, 0)
     sem = {}
@@ -410,56 +388,93 @@
                     v = v + into[e, rows].astype(F32)
                 fin[e, rows] = v.astype(BF16)
 
-    save = []
-
     def weight_grads(i):
         bit, zs = i // 4, i % 4
         tq = jnp.zeros((FEAT, TOK), F32)
-        tkv = jnp.zeros((FEAT, 64), F32)
+        tkv = jnp.zeros((64, FEAT), F32)
         for d in (0, 1):
             xs = 2 * d + lax.rem(bit + d + zl, 2)
             for e in (0, 1):
                 xb = X[e, xs, zs]
                 tq = tq + dot(xb, Gq[e, d], 0, 0)
-                tkv = tkv + dot(xb, Gkv[e, d], 0, 0)
-        wgq[i] = tq
+                tkv = tkv + dot(Gkv[e, d], xb, 0, 0)
+        wgq[i] = tq.astype(BF16)
         wgkv[i] = tkv
         save.append(local(wgq.at[i], gq_out.at[pl.ds(i * FEAT, FEAT)]))
-        save.append(local(wgkv.at[i], gkv_out.at[pl.ds(i * FEAT, FEAT)]))
-
+        save.append(local(wgkv.at[i], gkv_out.at[:, pl.ds(i * FEAT, FEAT)]))
+
+    def fars(e):
+        for i in range(4):
+            scatter_far(e, i)
+
+    def nears(e):
+        for i in range(4):
+            scatter_near(e, i)
+
+    stage0(False)
+    gather_first(0)
+    load_wq.wait()
+    load_wkv.wait()
+    gather_second(0)
+    gather_third(0)
+    arrived(X.at[1, x, zh], s1r, swap1)
+    gather_first(1)
+    for k in ORDER:
+        gather_near(0, k)
+    gather_second(1)
+    gather_third(1)
+    project_near(0)
+    for k in ORDER:
+        gather_far(0, k)
+    project_far(0)
+    send_partial(0)
+    gather_near(1, 0)
+    gather_near(1, -1)
+    send_kv(0)
+    gather_near(1, 1)
+    gather_near(1, 2)
+    attend(0)
+    project_near(1)
+    send_gkv(0)
+    for k in ORDER:
+        gather_far(1, k)
+    project_far(1)
+    send_partial(1)
+    take_g(0)
+    fars(0)
+    send_kv(1)
+    nears(0)
+    attend(1)
+    scatter_own(0, 0)
+    send_gkv(1)
+    scatter_own(0, 1)
+    take_g(1)
+    fars(1)
+    scatter_own(0, 2)
+    scatter_own(0, 3)
+    f1r = rr.at[take("r")]
+
+    def final0(start):
+        @pl.when(own)
+        def _():
+            keep(fin.at[0], hg_out.at[0], start)
+
+        @pl.when(jnp.logical_not(own))
+        def _():
+            swap(fin.at[0], hg_out.at[0], start)
+
+    final0(True)
     for i in range(4):
-        for e in (0, 1):
-            scatter_far(e, i)
-    for i in range(4):
-        for e in (0, 1):
-            scatter_near(e, i)
         weight_grads(i)
+    nears(1)
     for i in range(4):
         weight_grads(4 + i)
-        for e in (0, 1):
-            scatter_own(e, i)
-
-    f1r = rr.at[take("r")]
+    for i in range(4):
+        scatter_own(1, i)
     send(fin.at[1], hg_out.at[1], f1r, swap1)
-    f0s, f0r, f0l = ss.at[take("s")], rr.at[take("r")], ls.at[take("l")]
-
-    @pl.when(own)
-    def _():
-        copy = pltpu.make_async_copy(fin.at[0], hg_out.at[0], f0l)
-        copy.start()
-        copy.wait()
-
-    @pl.when(jnp.logical_not(own))
-    def _():
-        copy = pltpu.make_async_remote_copy(
-            src_ref=fin.at[0], dst_ref=hg_out.at[0], send_sem=f0s, recv_sem=f0r, device_id=swap0, device_id_type=MESH
-        )
-        copy.start()
-        copy.wait()
-
+    final0(False)
     arrived(hg_out.at[1], f1r, swap1)
-    arrived(att_out.at[1], ar[0], mirror)
-    save_att.wait()
+    arrived(att_out.at[1], ar, mirror)
     for copy in save:
         copy.wait()
     for copy in pending:
@@ -486,18 +501,18 @@
     nf = len(FLOWS)
     scratch = [
         V((2, 4, 4, TOK, FEAT), BF16),
-        V((4096, 256), BF16), V((4096, 64), BF16),
+        V((4096, 256), BF16), V((64, 4096), BF16),
         V((2, TOK, 256), BF16), V((1, TOK), jnp.int32),
         V((2, 2, TOK, 256), F32), V((2, 2, TOK, 64), F32),
         V((2, TOK, 256), BF16), V((2, 128, 128), BF16), V((2, TOK, 256), BF16), V((2, 128, 128), BF16),
         V((2, 4, 128, 128), BF16),
         V((2, 4, 128, 128), F32), V((2, 4, 128, 128), BF16), V((2, 3, 128, 128), BF16),
         V((2, 2, TOK, 256), BF16), V((2, 2, 128, 128), BF16), V((2, 2, TOK, 64), BF16),
-        V((2, 2, TOK, HEAD), BF16), V((2, TOK, HEAD), BF16), V((2, TOK, HEAD), BF16),
+        V((2, 2, TOK, HEAD), BF16),
         V((2, TOK, 256), BF16),
         big, big, big, big, big, big,
         mid, mid, mid, mid, mid, mid, mid,
-        V((8, FEAT, 256), F32), V((8, FEAT, 64), F32),
+        V((8, FEAT, 256), BF16), V((8, 64, FEAT), F32),
         pltpu.SemaphoreType.DMA((64 + 96 * nf,)),
         pltpu.SemaphoreType.DMA((48 + 48 * nf,)),
         pltpu.SemaphoreType.DMA((nf, 2, 4, 4, 2)),
@@ -508,8 +523,8 @@
         out_shape=(
             jax.ShapeDtypeStruct((2, TOK, 256), BF16),
             jax.ShapeDtypeStruct((2, TOK, FEAT), BF16),
-            jax.ShapeDtypeStruct((4096, 256), F32),
-            jax.ShapeDtypeStruct((4096, 64), F32),
+            jax.ShapeDtypeStruct((4096, 256), BF16),
+            jax.ShapeDtypeStruct((64, 4096), F32),
         ),
         in_specs=[anywhere, anywhere, anywhere, vmem, anywhere, vmem, vmem],
         out_specs=(anywhere,) * 4,
@@ -517,8 +532,8 @@
         compiler_params=pltpu.CompilerParams(
             collective_id=0, has_side_effects=True, vmem_limit_bytes=60 * 2**20
         ),
-    )(hidden[0], query_weight[0], keyval_weight[0], doc_ids[0], cotangent[0], cosf, sinf)
-    return att[None], hg[None], gq[None], gkv[None]
+    )(hidden[0], query_weight[0], keyval_weight[0].swapaxes(1, 2), doc_ids[0], cotangent[0], cosf, sinf)
+    return att[None], hg[None], gq.astype(F32)[None], gkv.T[None]
 
 
 def solution(mesh):

time: 250 us -> 209 us (0.84)
  Pallas kernels: 232 us -> 200 us
  local copies, waits for them, and re-layouts: 13.9 us -> 2.48 us
  other arithmetic: 0 us -> 4.06 us
    pallas_call x1, Pallas kernels: 232 us -> 200 us  [body(): pl.pallas_call(kernel, out_shape=(jax.ShapeDtypeStruct((2, TOK, 256), BF1...]
    unnamed x5 -> x9, local copies, waits for them, and re-layouts: 13.9 us -> 2.48 us
    broadcast_in_dim x0 -> x1, other arithmetic: none -> 4.06 us  [body(): return (att[None], hg[None], gq.astype(F32)[None], gkv.T[None])]
where the time goes in v2:
time: 209 us; the launch traced here: 208 us
  Pallas kernels  200 us (96%)
  other arithmetic  4.06 us (2%)
  local copies, waits for them, and re-layouts  2.48 us (1%)
    pallas_call x1, Pallas kernels, body(): pl.pallas_call(kernel, out_shape=(jax.ShapeDtypeStruct((2, TOK, 256), BF1...  200 us

profile of v2, /device:TPU:31, one launch (start us, length us, event | category | flops | bytes accessed | tf_op | source)
XLA Modules:
  0.0 207.5 jit_solution(16748846930090327673)
XLA Ops:
  0.6 200.3 %shard_map.102 = (bf16[2,256,256]{2,1,0:T(8,128)(2,1)}, bf16[2,256,512]{2,1,0:T(8,128)(2,1)}, bf16[4096,256]{1,0:T(8,128)(2,1)}, f32[64,4096]{1,0:T(8,128)}) custom-call(bf16[2,256,512]{2,1,0:T(8,128)(2,1)} %bitcast.18, bf16[2,4096,256]{2,1,0:T(8,128)(2,1)} %bitcast.15, bf16[2,64,4096]{2,1,0:T(8,128)(2,1)} %bitcast.17, s32[2,1,256]{2,1,0:T(1,128)} %bitcast.22, ...), custom_call_target="tpu_custom_call" | custom-call | tf_op jit(solution)/shard_map/pallas_call | solution.py:521
  200.9 0.0 copy-start.2
  200.9 0.0 copy-start.1
  201.0 0.0 copy-start
  201.0 4.1 %bitcast_convert_fusion = f32[1,4096,256]{2,1,0:T(8,128)} fusion(bf16[4096,256]{1,0:T(8,128)(2,1)} %get-tuple-element.10), kind=kLoop, calls=%fused_computation | loop fusion | flops 1048576 | bytes 6291456 | tf_op jit(solution)/shard_map/broadcast_in_dim | solution.py:536
  205.0 0.0 copy-done.2
  205.0 0.7 copy.14
  205.7 0.0 copy-done.1
  205.7 0.8 copy.15
  206.5 0.0 copy-done
  206.5 1.0 copy.16
Async XLA Ops:
  200.9 4.1 %copy-start.2 = (bf16[2,256,256]{2,1,0:T(8,128)(2,1)S(1)}, bf16[2,256,256]{2,1,0:T(8,128)(2,1)}, u32[]{:S(2)}) copy-start(bf16[2,256,256]{2,1,0:T(8,128)(2,1)} %get-tuple-element.8) | copy-start | bytes 786436
  200.9 4.8 %copy-start.1 = (bf16[2,256,512]{2,1,0:T(8,128)(2,1)S(1)}, bf16[2,256,512]{2,1,0:T(8,128)(2,1)}, u32[]{:S(2)}) copy-start(bf16[2,256,512]{2,1,0:T(8,128)(2,1)} %get-tuple-element.9) | copy-start | bytes 1572868
  201.0 5.6 %copy-start = (f32[64,4096]{1,0:T(8,128)S(1)}, f32[64,4096]{1,0:T(8,128)}, u32[]{:S(2)}) copy-start(f32[64,4096]{1,0:T(8,128)} %get-tuple-element.11) | copy-start | bytes 3145732

commit v3 on v2

v3 whole, which is shorter than its diff:
```python
import jax
import jax.numpy as jnp
import numpy as np
from jax import lax
from jax.experimental import pallas as pl
from jax.experimental.pallas import tpu as pltpu
from jax.sharding import PartitionSpec as P

MESH = pl.DeviceIdType.MESH
HEAD = 128
TOK = 256
FEAT = 512
F32 = jnp.float32
BF16 = jnp.bfloat16
QUARTER = 2048


def dot(a, b, ca, cb):
    return lax.dot_general(a, b, (((ca,), (cb,)), ((), ())), preferred_element_type=F32)


def pack(v):
    return jnp.concatenate([v[: TOK // 2], v[TOK // 2 :]], axis=1)


def unpack(v):
    v = v.astype(F32)
    return jnp.concatenate([v[:, :64], v[:, 64:]], axis=0)


def kernel(
    hid, wq, wkv, doc, cot, cosf, sinf,
    att_out, hg_out, gq_out, gkv_out,
    X, Wq, Wkv, C, docs, Pq, Pkv, PkvP, sPq, sPkv, rPq, rPkv, KV, gfp, gsb, grb, Gq, Gkvp, Gkv, Qb, att,
    sd, rd, zsd, zsp, zsm, zrd, zrp, zrm, fin, wgq, wgkv,
    ss, rr, ra, ls,
):
    pipe, tens, zl = lax.axis_index("pipe"), lax.axis_index("tensor"), lax.axis_index("dp")
    x, zh = lax.div(tens, 4), lax.rem(tens, 4)
    y, c = lax.div(pipe, 2), lax.rem(pipe, 2)
    own = lax.div(x, 2) == zl

    def dev(x, y, zh, zl, c):
        return {"pipe": y * 2 + c, "tensor": x * 4 + zh, "dp": zl}

    def up(v, k):
        return lax.rem(v + k + 4, 4)

    zflip = 1 - zl
    xb = lax.rem(x, 2)
    xpair = x + 1 - 2 * xb
    held = lax.div(x, 2)
    qb = lax.rem(xb + held + zl, 2)
    neighbour = {
        1: dev(x, y, up(zh, 1), zl, c),
        -1: dev(x, y, up(zh, -1), zl, c),
        2: dev(x, y, up(zh, 2), zl, c),
    }
    across = dev(3 - x, y, zh, zl, c)
    pair = dev(xpair, y, zh, zl, c)
    square = (pair, dev(x, y, zh, zflip, c), dev(xpair, y, zh, zflip, c))
    mirror = dev(x, 3 - y, zh, zl, 1 - c)
    swap0 = dev(3 - x, y, zh, zflip, c)
    swap1 = dev(jnp.where(own, x, 3 - x), 3 - y, zh, jnp.where(own, zl, zflip), 1 - c)

    count = {"s": 0, "r": 0, "l": 0}
    pending = []
    save = []

    def take(kind):
        count[kind] += 1
        return count[kind] - 1

    def send(src, dst, rsem, to):
        copy = pltpu.make_async_remote_copy(
            src_ref=src, dst_ref=dst, send_sem=ss.at[take("s")], recv_sem=rsem, device_id=to, device_id_type=MESH
        )
        copy.start()
        pending.append(copy)

    def arrived(dst, rsem, frm):
        pltpu.make_async_remote_copy(
            src_ref=dst, dst_ref=dst, send_sem=ss.at[0], recv_sem=rsem, device_id=frm, device_id_type=MESH
        ).wait_recv()

    def local(src, dst):
        copy = pltpu.make_async_copy(src, dst, ls.at[take("l")])
        copy.start()
        return copy

    barrier = pltpu.get_barrier_semaphore()
    greet0 = dev(
        jnp.where(own, x, 3 - x), jnp.where(own, 3 - y, y), zh, jnp.where(own, zl, zflip), jnp.where(own, 1 - c, c)
    )
    for to in list(neighbour.values()) + [across, mirror, swap1, greet0] + list(square):
        pl.semaphore_signal(barrier, inc=1, device_id=to, device_id_type=MESH)
    pl.semaphore_wait(barrier, 10)

    s0s, s0r, s0l = ss.at[take("s")], rr.at[take("r")], ls.at[take("l")]

    def keep(src, dst, start):
        copy = pltpu.make_async_copy(src, dst, s0l)
        copy.start() if start else copy.wait()

    def swap(src, dst, start):
        copy = pltpu.make_async_remote_copy(
            src_ref=src, dst_ref=dst, send_sem=s0s, recv_sem=s0r, device_id=swap0, device_id_type=MESH
        )
        copy.start() if start else copy.wait()

    def stage0(start):
        @pl.when(own)
        def _():
            keep(hid.at[0], X.at[0, held, zh], start)

        @pl.when(jnp.logical_not(own))
        def _():
            swap(hid.at[0], X.at[0, 1 - held, zh], start)

    s1r, cr, dr = rr.at[take("r")], rr.at[take("r")], rr.at[take("r")]
    stage0(True)
    send(hid.at[1], X.at[1, jnp.where(own, held, 1 - held), zh], s1r, swap1)
    mine = pl.ds(pl.multiple_of(qb * QUARTER, QUARTER), QUARTER)
    theirs = pl.ds(pl.multiple_of((1 - qb) * QUARTER, QUARTER), QUARTER)
    load_wq = local(wq.at[0, mine], Wq.at[xb])
    load_wkv = local(wkv.at[0, :, mine], Wkv.at[xb])
    wr = (rr.at[take("r")], rr.at[take("r")])
    send(wq.at[0, theirs], Wq.at[xb], wr[0], pair)
    send(wkv.at[0, :, theirs], Wkv.at[xb], wr[1], pair)
    load_c = local(cot.at[0], C.at[0])
    send(cot.at[1], C.at[1], cr, mirror)
    send(doc.at[1], docs, dr, mirror)
    Pq[...] = jnp.zeros_like(Pq)
    Pkv[...] = jnp.zeros_like(Pkv)

    def features(zs):
        return pl.ds(pl.multiple_of(zs * FEAT, FEAT), FEAT)

    def kv_weights(rows):
        return Wkv[:, :, rows].reshape(HEAD, FEAT)

    def project(e, d, zs):
        rows = features(zs)
        block = X[e, d, zs]
        for s in (0, 1):
            Pq[e, d, s] += dot(block, Wq[s, rows, :], 1, 0)
        Pkv[e, d] += dot(block, kv_weights(rows), 1, 1)

    HALF = (pl.ds(0, TOK // 2), pl.ds(TOK // 2, TOK // 2))

    def pass_on(e, k, half, sign):
        ref = X.at[e, held, up(zh, k)]
        if half is not None:
            ref = ref.at[HALF[half]]
        send(ref, ref, ra.at[e, held, up(zh, k), half or 0], neighbour[sign])

    def got(e, k, half, sign):
        ref = X.at[e, held, up(zh, k)]
        if half is not None:
            ref = ref.at[HALF[half]]
        arrived(ref, ra.at[e, held, up(zh, k), half or 0], neighbour[sign])

    def share(e, k):
        ref = X.at[e, held, up(zh, k)]
        send(ref, ref, ra.at[e, held, up(zh, k), 0], across)

    def shared(e, k):
        ref = X.at[e, 1 - held, up(zh, k)]
        arrived(ref, ra.at[e, 1 - held, up(zh, k), 0], across)

    def gather_first(e):
        pass_on(e, 0, None, 1)
        pass_on(e, 0, None, -1)
        share(e, 0)

    def gather_second(e):
        got(e, -1, None, -1)
        pass_on(e, -1, 0, 1)
        share(e, -1)
        got(e, 1, None, 1)
        pass_on(e, 1, 1, -1)
        share(e, 1)

    def gather_third(e):
        got(e, 2, 0, -1)
        got(e, 2, 1, 1)
        share(e, 2)

    ORDER = (0, -1, 1, 2)

    def project_held(e):
        for k in ORDER:
            project(e, held, up(zh, k))

    def project_shared(e):
        for k in ORDER:
            shared(e, k)
            project(e, 1 - held, up(zh, k))

    cosw, sinw = cosf[...], sinf[...]

    def rope(v):
        return v * cosw + pltpu.roll(v, 64, 1) * sinw

    def unrope(v):
        return v * cosw - pltpu.roll(v, 64, 1) * sinw

    zto = {1: neighbour[1], 2: neighbour[2], 3: neighbour[-1]}
    zfrom = {1: neighbour[-1], 2: neighbour[2], 3: neighbour[1]}

    def three():
        return [[rr.at[take("r")] for _ in range(3)] for e in (0, 1)]

    prq, prk, kvr, gr, xrq, xrk = three(), three(), three(), three(), three(), three()
    ar = rr.at[take("r")]
    members = ((zl, 1 - xb), (zflip, xb), (zflip, 1 - xb))
    scale = HEAD**-0.5

    def send_partial(e):
        for d in (0, 1):
            for s in (0, 1):
                PkvP[e, d, s] = pack(Pkv[e, d, :, 64 * s : 64 * s + 64])
        for i, (d, s) in enumerate(members):
            sPkv[e, i] = PkvP[e, d, s].astype(BF16)
            send(sPkv.at[e, i], rPkv.at[e, i], prk[e][i], square[i])
        for i, (d, s) in enumerate(members):
            sPq[e, i] = Pq[e, d, s].astype(BF16)
            send(sPq.at[e, i], rPq.at[e, i], prq[e][i], square[i])

    def send_kv(e):
        piece = PkvP[e, zl, xb]
        for i in range(3):
            arrived(rPkv.at[e, i], prk[e][i], square[i])
            piece = piece + rPkv[e, i].astype(F32)
        KV[e, zh] = piece.astype(BF16)
        for o in (1, 2, 3):
            send(KV.at[e, zh], KV.at[e, zh], kvr[e][o - 1], zto[o])
        q = Pq[e, zl, xb]
        for i in range(3):
            arrived(rPq.at[e, i], prq[e][i], square[i])
            q = q + rPq[e, i].astype(F32)
        Qb[e, 0] = rope(q[:, :HEAD]).astype(BF16)
        Qb[e, 1] = rope(q[:, HEAD:]).astype(BF16)

    def attend(e):
        if e == 0:
            load_c.wait()
        else:
            arrived(C.at[1], cr, mirror)
            arrived(docs, dr, mirror)
        row = lax.broadcasted_iota(jnp.int32, (TOK, TOK), 0)
        col = lax.broadcasted_iota(jnp.int32, (TOK, TOK), 1)
        ids = doc[0] if e == 0 else docs[...]
        wide = jnp.broadcast_to(ids.astype(F32), (TOK, TOK))
        allowed = (wide == wide.T) & (col <= row)
        for o in (1, 2, 3):
            arrived(KV.at[e, up(zh, -o)], kvr[e][o - 1], zfrom[o])
        kraw = jnp.concatenate([unpack(KV[e, 0]), unpack(KV[e, 1])], axis=1)
        keys = rope(kraw).astype(BF16)
        values = jnp.concatenate([unpack(KV[e, 2]), unpack(KV[e, 3])], axis=1).astype(BF16)
        gk = jnp.zeros((TOK, HEAD), F32)
        gv = jnp.zeros((TOK, HEAD), F32)
        for j in (0, 1):
            q = Qb[e, j]
            g = C[e, :, j * HEAD : (j + 1) * HEAD]
            weights = jnp.where(allowed, jnp.exp(dot(q, keys, 1, 1) * scale), 0.0)
            probs = weights / jnp.sum(weights, axis=-1, keepdims=True)
            low = probs.astype(BF16)
            att[e, :, j * HEAD : (j + 1) * HEAD] = dot(low, values, 1, 0).astype(BF16)
            gv = gv + dot(low, g, 0, 0)
            gp = dot(g, values, 1, 1)
            rdot = jnp.sum(gp * probs, axis=-1, keepdims=True)
            gs = (probs * (gp - rdot) * scale).astype(BF16)
            Gq[e, zl, xb, :, j * HEAD : (j + 1) * HEAD] = unrope(dot(gs, keys, 1, 0)).astype(BF16)
            gk = gk + dot(gs, q, 0, 0)
        gk = unrope(gk)
        for i, v in enumerate((gk[:, :64], gk[:, 64:], gv[:, :64], gv[:, 64:])):
            v = pack(v)
            gfp[e, i] = v
            gsb[e, i] = v.astype(BF16)
        for o in (1, 2, 3):
            send(gsb.at[e, up(zh, o)], grb.at[e, o - 1], gr[e][o - 1], zto[o])
        for i in range(3):
            send(Gq.at[e, zl, xb], Gq.at[e, zl, xb], xrq[e][i], square[i])
        if e == 0:
            save.append(local(att.at[0], att_out.at[0]))
        else:
            send(att.at[1], att_out.at[1], ar, mirror)

    def send_gkv(e):
        total = gfp[e, zh]
        for o in (1, 2, 3):
            arrived(grb.at[e, o - 1], gr[e][o - 1], zfrom[o])
            total = total + grb[e, o - 1].astype(F32)
        Gkvp[e, zl, xb] = total.astype(BF16)
        for i in range(3):
            send(Gkvp.at[e, zl, xb], Gkvp.at[e, zl, xb], xrk[e][i], square[i])

    def take_g(e):
        for i, (d, s) in enumerate(members):
            arrived(Gq.at[e, d, s], xrq[e][i], square[i])
            arrived(Gkvp.at[e, d, s], xrk[e][i], square[i])
        for d in (0, 1):
            Gkv[e, d] = jnp.concatenate([unpack(Gkvp[e, d, 0]), unpack(Gkvp[e, d, 1])], axis=1).astype(BF16)

    def term(e, d, zs):
        rows = features(zs)
        v = dot(Gkv[e, d], kv_weights(rows), 1, 0)
        for s in (0, 1):
            v = v + dot(Gq[e, d, s], Wq[s, rows, :], 1, 1)
        return v

    BACK = (2, 1, -1, 0)
    xs_r = [[rr.at[take("r")] for _ in BACK] for e in (0, 1)]
    zdr = [[rr.at[take("r")] for _ in (0, 1)] for e in (0, 1)]
    znr = [[rr.at[take("r")] for _ in (0, 1)] for e in (0, 1)]

    def fars(e):
        for i, k in enumerate(BACK):
            sd[e, i] = term(e, 1 - held, up(zh, k)).astype(BF16)
            send(sd.at[e, i], rd.at[e, i], xs_r[e][i], across)

    def add_half(v, other, half):
        n = TOK // 2
        other = other.astype(F32)
        if half == 0:
            return jnp.concatenate([v[:n] + other, v[n:]], axis=0)
        return jnp.concatenate([v[:n], v[n:] + other], axis=0)

    def scatter_own(e, i):
        k = BACK[i]
        v = term(e, held, up(zh, k))
        arrived(rd.at[e, i], xs_r[e][i], across)
        v = v + rd[e, i].astype(F32)
        if k == 2:
            zsd[e] = v.astype(BF16)
            for half, sign in ((0, 1), (1, -1)):
                send(zsd.at[e, HALF[half]], zrd.at[e, HALF[half]], zdr[e][half], neighbour[sign])
        elif k in (1, -1):
            half, out, into = (0, zsp, zrp) if k == 1 else (1, zsm, zrm)
            arrived(zrd.at[e, HALF[half]], zdr[e][half], neighbour[-k])
            v = add_half(v, zrd[e, HALF[half]], half)
            out[e] = v.astype(BF16)
            send(out.at[e], into.at[e], znr[e][half], neighbour[k])
        else:
            for half, sign, into in ((0, 1, zrp), (1, -1, zrm)):
                arrived(into.at[e], znr[e][half], neighbour[-sign])
                v = v + into[e].astype(F32)
            fin[e] = v.astype(BF16)

    wsr = [(rr.at[take("r")], rr.at[take("r")]) for _ in range(4)]

    def rows_out(zs, quarter):
        start = quarter * QUARTER + zs * FEAT
        return pl.ds(pl.multiple_of(start, FEAT), FEAT)

    def query_grads(zs, s):
        t = jnp.zeros((FEAT, TOK), F32)
        for e in (0, 1):
            for d in (0, 1):
                t = t + dot(X[e, d, zs], Gq[e, d, s], 0, 0)
        return t.astype(BF16)

    def weight_grads_pair(zs):
        rows = rows_out(zs, qb)
        wgq[1, zs] = query_grads(zs, 1 - xb)
        send(wgq.at[1, zs], gq_out.at[rows], wsr[zs][0], pair)
        t = jnp.zeros((HEAD, FEAT), F32)
        for e in (0, 1):
            for d in (0, 1):
                t = t + dot(Gkv[e, d], X[e, d, zs], 0, 0)
        wgkv[zs] = t.astype(BF16).reshape(2, 64, FEAT)
        send(wgkv.at[zs, 1 - xb], gkv_out.at[:, rows], wsr[zs][1], pair)
        save.append(local(wgkv.at[zs, xb], gkv_out.at[:, rows]))

    def weight_grads_own(zs):
        wgq[0, zs] = query_grads(zs, xb)
        save.append(local(wgq.at[0, zs], gq_out.at[rows_out(zs, qb)]))

    f1r = rr.at[take("r")]

    def final0(start):
        @pl.when(own)
        def _():
            keep(fin.at[0], hg_out.at[0], start)

        @pl.when(jnp.logical_not(own))
        def _():
            swap(fin.at[0], hg_out.at[0], start)

    stage0(False)
    gather_first(0)
    gather_second(0)
    gather_third(0)
    arrived(X.at[1, held, zh], s1r, swap1)
    gather_first(1)
    load_wq.wait()
    load_wkv.wait()
    arrived(Wq.at[1 - xb], wr[0], pair)
    arrived(Wkv.at[1 - xb], wr[1], pair)
    project_held(0)
    project_shared(0)
    send_partial(0)
    gather_second(1)
    send_kv(0)
    gather_third(1)
    attend(0)
    project_held(1)
    send_gkv(0)
    project_shared(1)
    send_partial(1)
    take_g(0)
    fars(0)
    send_kv(1)
    scatter_own(0, 0)
    attend(1)
    scatter_own(0, 1)
    scatter_own(0, 2)
    send_gkv(1)
    scatter_own(0, 3)
    final0(True)
    take_g(1)
    fars(1)
    for zs in range(4):
        weight_grads_pair(zs)
        scatter_own(1, zs)
    send(fin.at[1], hg_out.at[1], f1r, swap1)
    for zs in range(4):
        weight_grads_own(zs)
    final0(False)
    arrived(hg_out.at[1], f1r, swap1)
    arrived(att_out.at[1], ar, mirror)
    for zs in range(4):
        rows = rows_out(zs, 1 - qb)
        arrived(gq_out.at[rows], wsr[zs][0], pair)
        arrived(gkv_out.at[:, rows], wsr[zs][1], pair)
    for copy in save:
        copy.wait()
    for copy in pending:
        copy.wait_send()


def rope_tables():
    freqs = 10000.0 ** (-2.0 * np.arange(HEAD // 2) / HEAD)
    angles = np.arange(TOK, dtype=np.float32)[:, None] * freqs.astype(np.float32)[None, :]
    cosine, sine = np.cos(angles), np.sin(angles)
    return (
        np.concatenate([cosine, cosine], 1).astype(np.float32),
        np.concatenate([-sine, sine], 1).astype(np.float32),
    )


def body(hidden, query_weight, keyval_weight, doc_ids, cotangent):
    cosf, sinf = rope_tables()
    anywhere = pl.BlockSpec(memory_space=pl.ANY)
    vmem = pl.BlockSpec(memory_space=pltpu.VMEM)
    V = pltpu.VMEM
    big = V((2, 4, TOK, FEAT), BF16)
    mid = V((2, TOK, FEAT), BF16)
    scratch = [
        V((2, 2, 4, TOK, FEAT), BF16),
        V((2, QUARTER, 256), BF16), V((2, 64, QUARTER), BF16),
        V((2, TOK, 256), BF16), V((1, TOK), jnp.int32),
        V((2, 2, 2, TOK, 256), F32), V((2, 2, TOK, 128), F32), V((2, 2, 2, 128, 128), F32),
        V((2, 3, TOK, 256), BF16), V((2, 3, 128, 128), BF16), V((2, 3, TOK, 256), BF16), V((2, 3, 128, 128), BF16),
        V((2, 4, 128, 128), BF16),
        V((2, 4, 128, 128), F32), V((2, 4, 128, 128), BF16), V((2, 3, 128, 128), BF16),
        V((2, 2, 2, TOK, 256), BF16), V((2, 2, 2, 128, 128), BF16), V((2, 2, TOK, 128), BF16),
        V((2, 2, TOK, HEAD), BF16),
        V((2, TOK, 256), BF16),
        big, big,
        mid, mid, mid, mid, mid, mid, mid,
        V((2, 4, FEAT, 256), BF16), V((4, 2, 64, FEAT), BF16),
        pltpu.SemaphoreType.DMA((112,)),
        pltpu.SemaphoreType.DMA((96,)),
        pltpu.SemaphoreType.DMA((2, 2, 4, 2)),
        pltpu.SemaphoreType.DMA((32,)),
    ]
    att, hg, gq, gkv = pl.pallas_call(
        kernel,
        out_shape=(
            jax.ShapeDtypeStruct((2, TOK, 256), BF16),
            jax.ShapeDtypeStruct((2, TOK, FEAT), BF16),
            jax.ShapeDtypeStruct((4096, 256), BF16),
            jax.ShapeDtypeStruct((64, 4096), BF16),
        ),
        in_specs=[anywhere, anywhere, anywhere, vmem, anywhere, vmem, vmem],
        out_specs=(anywhere,) * 4,
        scratch_shapes=scratch,
        compiler_params=pltpu.CompilerParams(
            collective_id=0, has_side_effects=True, vmem_limit_bytes=60 * 2**20
        ),
    )(hidden[0], query_weight[0], keyval_weight[0].swapaxes(1, 2), doc_ids[0], cotangent[0], cosf, sinf)
    return att[None], hg[None], gq.astype(F32)[None], gkv.astype(F32).T[None]


def solution(mesh):
    sharded = P("pipe", None, "dp", "tensor")
    return jax.shard_map(
        body,
        mesh=mesh,
        in_specs=(sharded, sharded, sharded, P("pipe", None, "dp", None), sharded),
        out_specs=(sharded, sharded, P("pipe", "dp", "tensor"), P("pipe", "dp", "tensor")),
        check_vma=False,
    )
```

time: 209 us -> 173 us (0.83)
  Pallas kernels: 200 us -> 165 us
    pallas_call x1, Pallas kernels: 200 us -> 165 us  [body(): pl.pallas_call(kernel, out_shape=(jax.ShapeDtypeStruct((2, TOK, 256), BF1...]
    broadcast_in_dim x1 -> x2, other arithmetic: 4.06 us -> 5.07 us  [body(): return (att[None], hg[None], gq.astype(F32)[None], gkv.astype(F32).T[None])]
where the time goes in v3:
time: 173 us; the launch traced here: 172 us
  Pallas kernels  165 us (95%)
  other arithmetic  5.07 us (3%)
    pallas_call x1, Pallas kernels, body(): pl.pallas_call(kernel, out_shape=(jax.ShapeDtypeStruct((2, TOK, 256), BF1...  165 us
    broadcast_in_dim x2, other arithmetic, body(): return (att[None], hg[None], gq.astype(F32)[None], gkv.astype(F32).T[None])  5.07 us

profile of v3, /device:TPU:31, one launch (start us, length us, event | category | flops | bytes accessed | tf_op | source)
XLA Modules:
  0.0 172.3 jit_solution(12763402141451891860)
XLA Ops:
  0.6 165.1 %shard_map.102 = (bf16[2,256,256]{2,1,0:T(8,128)(2,1)}, bf16[2,256,512]{2,1,0:T(8,128)(2,1)}, bf16[4096,256]{1,0:T(8,128)(2,1)}, bf16[64,4096]{1,0:T(8,128)(2,1)}) custom-call(bf16[2,256,512]{2,1,0:T(8,128)(2,1)} %bitcast.18, bf16[2,4096,256]{2,1,0:T(8,128)(2,1)} %bitcast.16, bf16[2,64,4096]{2,1,0:T(8,128)(2,1)} %bitcast.17, s32[2,1,256]{2,1,0:T(1,128)} %bitcast.22, ...), custom_call_target="tpu_custom_call" | custom-call | tf_op jit(solution)/shard_map/pallas_call | solution.py:479
  165.7 0.0 copy-start
  165.7 0.0 copy-start.2
  165.7 0.0 copy-start.1
  165.8 4.0 %bitcast_convert_fusion = f32[1,4096,256]{2,1,0:T(8,128)} fusion(bf16[4096,256]{1,0:T(8,128)(2,1)} %get-tuple-element.10), kind=kLoop, calls=%fused_computation | loop fusion | flops 1048576 | bytes 6291456 | tf_op jit(solution)/shard_map/broadcast_in_dim | solution.py:494
  169.8 0.0 copy-done
  169.8 1.0 convert_bitcast_fusion
  170.8 0.0 copy-done.2
  170.8 0.7 copy.13
  171.5 0.0 copy-done.1
  171.5 0.8 copy.14
Async XLA Ops:
  165.7 4.1 %copy-start = (bf16[64,4096]{1,0:T(8,128)(2,1)S(1)}, bf16[64,4096]{1,0:T(8,128)(2,1)}, u32[]{:S(2)}) copy-start(bf16[64,4096]{1,0:T(8,128)(2,1)} %get-tuple-element.11) | copy-start | bytes 1572868
  165.7 5.1 %copy-start.2 = (bf16[2,256,256]{2,1,0:T(8,128)(2,1)S(1)}, bf16[2,256,256]{2,1,0:T(8,128)(2,1)}, u32[]{:S(2)}) copy-start(bf16[2,256,256]{2,1,0:T(8,128)(2,1)} %get-tuple-element.8) | copy-start | bytes 786436
  165.7 5.8 %copy-start.1 = (bf16[2,256,512]{2,1,0:T(8,128)(2,1)S(1)}, bf16[2,256,512]{2,1,0:T(8,128)(2,1)}, u32[]{:S(2)}) copy-start(bf16[2,256,512]{2,1,0:T(8,128)(2,1)} %get-tuple-element.9) | copy-start | bytes 1572868

commit v4 on v3

--- a/solution.py
+++ b/solution.py
@@ -13,6 +13,7 @@
 F32 = jnp.float32
 BF16 = jnp.bfloat16
 QUARTER = 2048
+PART = TOK // 2
 
 
 def dot(a, b, ca, cb):
@@ -31,7 +32,7 @@
 def kernel(
     hid, wq, wkv, doc, cot, cosf, sinf,
     att_out, hg_out, gq_out, gkv_out,
-    X, Wq, Wkv, C, docs, Pq, Pkv, PkvP, sPq, sPkv, rPq, rPkv, KV, gfp, gsb, grb, Gq, Gkvp, Gkv, Qb, att,
+    X, relay, Wq, Wkv, C, docs, Pq, Pkv, PkvP, sPq, sPkv, rPq, rPkv, KV, gfp, gsb, grb, Gq, Gkvp, Gkv, Qb, att,
     sd, rd, zsd, zsp, zsm, zrd, zrp, zrm, fin, wgq, wgkv,
     ss, rr, ra, ls,
 ):
@@ -92,34 +93,54 @@
     greet0 = dev(
         jnp.where(own, x, 3 - x), jnp.where(own, 3 - y, y), zh, jnp.where(own, zl, zflip), jnp.where(own, 1 - c, c)
     )
-    for to in list(neighbour.values()) + [across, mirror, swap1, greet0] + list(square):
+    for to in [neighbour[1], neighbour[-1], across, mirror, greet0] + list(square):
         pl.semaphore_signal(barrier, inc=1, device_id=to, device_id_type=MESH)
-    pl.semaphore_wait(barrier, 10)
-
-    s0s, s0r, s0l = ss.at[take("s")], rr.at[take("r")], ls.at[take("l")]
-
-    def keep(src, dst, start):
-        copy = pltpu.make_async_copy(src, dst, s0l)
-        copy.start() if start else copy.wait()
-
-    def swap(src, dst, start):
-        copy = pltpu.make_async_remote_copy(
-            src_ref=src, dst_ref=dst, send_sem=s0s, recv_sem=s0r, device_id=swap0, device_id_type=MESH
-        )
-        copy.start() if start else copy.wait()
-
-    def stage0(start):
+    pl.semaphore_wait(barrier, 8)
+
+    def part(h):
+        return pl.ds(h * PART, PART)
+
+    s0s = [ss.at[take("s")] for _ in (0, 1)]
+    s0r = [rr.at[take("r")] for _ in (0, 1)]
+    s0l = [ls.at[take("l")] for _ in (0, 1)]
+
+    def swap(src, dst_own, dst, h, start):
         @pl.when(own)
         def _():
-            keep(hid.at[0], X.at[0, held, zh], start)
+            copy = pltpu.make_async_copy(src.at[part(h)], dst_own.at[part(h)], s0l[h])
+            copy.start() if start else copy.wait()
 
         @pl.when(jnp.logical_not(own))
         def _():
-            swap(hid.at[0], X.at[0, 1 - held, zh], start)
+            copy = pltpu.make_async_remote_copy(
+                src_ref=src.at[part(h)], dst_ref=dst.at[part(h)], send_sem=s0s[h], recv_sem=s0r[h],
+                device_id=swap0, device_id_type=MESH,
+            )
+            copy.start() if start else copy.wait()
+
+    def stage0(h, start):
+        swap(hid.at[0], X.at[0, held, zh], X.at[0, 1 - held, zh], h, start)
 
     s1r, cr, dr = rr.at[take("r")], rr.at[take("r")], rr.at[take("r")]
-    stage0(True)
-    send(hid.at[1], X.at[1, jnp.where(own, held, 1 - held), zh], s1r, swap1)
+    stage0(0, True)
+    stage0(1, True)
+    send(hid.at[1], relay, s1r, mirror)
+    s2s, s2r, s2l = ss.at[take("s")], rr.at[take("r")], ls.at[take("l")]
+
+    def stage1(start):
+        @pl.when(own)
+        def _():
+            copy = pltpu.make_async_copy(relay, X.at[1, held, zh], s2l)
+            copy.start() if start else copy.wait()
+
+        @pl.when(jnp.logical_not(own))
+        def _():
+            copy = pltpu.make_async_remote_copy(
+                src_ref=relay, dst_ref=X.at[1, 1 - held, zh], send_sem=s2s, recv_sem=s2r,
+                device_id=swap0, device_id_type=MESH,
+            )
+            copy.start() if start else copy.wait()
+
     mine = pl.ds(pl.multiple_of(qb * QUARTER, QUARTER), QUARTER)
     theirs = pl.ds(pl.multiple_of((1 - qb) * QUARTER, QUARTER), QUARTER)
     load_wq = local(wq.at[0, mine], Wq.at[xb])
@@ -146,45 +167,48 @@
             Pq[e, d, s] += dot(block, Wq[s, rows, :], 1, 0)
         Pkv[e, d] += dot(block, kv_weights(rows), 1, 1)
 
-    HALF = (pl.ds(0, TOK // 2), pl.ds(TOK // 2, TOK // 2))
-
-    def pass_on(e, k, half, sign):
-        ref = X.at[e, held, up(zh, k)]
-        if half is not None:
-            ref = ref.at[HALF[half]]
-        send(ref, ref, ra.at[e, held, up(zh, k), half or 0], neighbour[sign])
-
-    def got(e, k, half, sign):
-        ref = X.at[e, held, up(zh, k)]
-        if half is not None:
-            ref = ref.at[HALF[half]]
-        arrived(ref, ra.at[e, held, up(zh, k), half or 0], neighbour[sign])
-
-    def share(e, k):
-        ref = X.at[e, held, up(zh, k)]
-        send(ref, ref, ra.at[e, held, up(zh, k), 0], across)
+    def cut(h, half):
+        if half is None:
+            return part(h)
+        return pl.ds(h * PART + half * (PART // 2), PART // 2)
+
+    def slot(e, h, d, k, half):
+        return X.at[e, d, up(zh, k), cut(h, half)], ra.at[e, h, d, up(zh, k), half or 0]
+
+    def pass_on(e, h, k, half, sign):
+        ref, sem = slot(e, h, held, k, half)
+        send(ref, ref, sem, neighbour[sign])
+
+    def got(e, h, k, half, sign):
+        ref, sem = slot(e, h, held, k, half)
+        arrived(ref, sem, neighbour[sign])
+
+    def share(e, h, k):
+        ref, sem = slot(e, h, held, k, None)
+        send(ref, ref, sem, across)
 
     def shared(e, k):
-        ref = X.at[e, 1 - held, up(zh, k)]
-        arrived(ref, ra.at[e, 1 - held, up(zh, k), 0], across)
-
-    def gather_first(e):
-        pass_on(e, 0, None, 1)
-        pass_on(e, 0, None, -1)
-        share(e, 0)
-
-    def gather_second(e):
-        got(e, -1, None, -1)
-        pass_on(e, -1, 0, 1)
-        share(e, -1)
-        got(e, 1, None, 1)
-        pass_on(e, 1, 1, -1)
-        share(e, 1)
-
-    def gather_third(e):
-        got(e, 2, 0, -1)
-        got(e, 2, 1, 1)
-        share(e, 2)
+        for h in (0, 1):
+            ref, sem = slot(e, h, 1 - held, k, None)
+            arrived(ref, sem, across)
+
+    def gather_first(e, h):
+        pass_on(e, h, 0, None, 1)
+        pass_on(e, h, 0, None, -1)
+        share(e, h, 0)
+
+    def gather_second(e, h):
+        got(e, h, -1, None, -1)
+        pass_on(e, h, -1, 0, 1)
+        share(e, h, -1)
+        got(e, h, 1, None, 1)
+        pass_on(e, h, 1, 1, -1)
+        share(e, h, 1)
+
+    def gather_third(e, h):
+        got(e, h, 2, 0, -1)
+        got(e, h, 2, 1, 1)
+        share(e, h, 2)
 
     ORDER = (0, -1, 1, 2)
 
@@ -303,50 +327,53 @@
         for d in (0, 1):
             Gkv[e, d] = jnp.concatenate([unpack(Gkvp[e, d, 0]), unpack(Gkvp[e, d, 1])], axis=1).astype(BF16)
 
-    def term(e, d, zs):
+    def term(e, d, zs, h):
         rows = features(zs)
-        v = dot(Gkv[e, d], kv_weights(rows), 1, 0)
+        v = dot(Gkv[e, d, part(h)], kv_weights(rows), 1, 0)
         for s in (0, 1):
-            v = v + dot(Gq[e, d, s], Wq[s, rows, :], 1, 1)
+            v = v + dot(Gq[e, d, s, part(h)], Wq[s, rows, :], 1, 1)
         return v
 
     BACK = (2, 1, -1, 0)
-    xs_r = [[rr.at[take("r")] for _ in BACK] for e in (0, 1)]
-    zdr = [[rr.at[take("r")] for _ in (0, 1)] for e in (0, 1)]
-    znr = [[rr.at[take("r")] for _ in (0, 1)] for e in (0, 1)]
+
+    def sems(n):
+        return [[[rr.at[take("r")] for _ in range(n)] for h in (0, 1)] for e in (0, 1)]
+
+    xs_r, zdr, znr = sems(4), sems(2), sems(2)
 
     def fars(e):
         for i, k in enumerate(BACK):
-            sd[e, i] = term(e, 1 - held, up(zh, k)).astype(BF16)
-            send(sd.at[e, i], rd.at[e, i], xs_r[e][i], across)
+            for h in (0, 1):
+                sd[e, i, part(h)] = term(e, 1 - held, up(zh, k), h).astype(BF16)
+                send(sd.at[e, i, part(h)], rd.at[e, i, part(h)], xs_r[e][h][i], across)
 
     def add_half(v, other, half):
-        n = TOK // 2
+        n = PART // 2
         other = other.astype(F32)
         if half == 0:
             return jnp.concatenate([v[:n] + other, v[n:]], axis=0)
         return jnp.concatenate([v[:n], v[n:] + other], axis=0)
 
-    def scatter_own(e, i):
-        k = BACK[i]
-        v = term(e, held, up(zh, k))
-        arrived(rd.at[e, i], xs_r[e][i], across)
-        v = v + rd[e, i].astype(F32)
+    def scatter_own(e, h, i):
+        k, rows = BACK[i], part(h)
+        v = term(e, held, up(zh, k), h)
+        arrived(rd.at[e, i, rows], xs_r[e][h][i], across)
+        v = v + rd[e, i, rows].astype(F32)
         if k == 2:
-            zsd[e] = v.astype(BF16)
+            zsd[e, rows] = v.astype(BF16)
             for half, sign in ((0, 1), (1, -1)):
-                send(zsd.at[e, HALF[half]], zrd.at[e, HALF[half]], zdr[e][half], neighbour[sign])
+                send(zsd.at[e, cut(h, half)], zrd.at[e, cut(h, half)], zdr[e][h][half], neighbour[sign])
         elif k in (1, -1):
             half, out, into = (0, zsp, zrp) if k == 1 else (1, zsm, zrm)
-            arrived(zrd.at[e, HALF[half]], zdr[e][half], neighbour[-k])
-            v = add_half(v, zrd[e, HALF[half]], half)
-            out[e] = v.astype(BF16)
-            send(out.at[e], into.at[e], znr[e][half], neighbour[k])
+            arrived(zrd.at[e, cut(h, half)], zdr[e][h][half], neighbour[-k])
+            v = add_half(v, zrd[e, cut(h, half)], half)
+            out[e, rows] = v.astype(BF16)
+            send(out.at[e, rows], into.at[e, rows], znr[e][h][half], neighbour[k])
         else:
             for half, sign, into in ((0, 1, zrp), (1, -1, zrm)):
-                arrived(into.at[e], znr[e][half], neighbour[-sign])
-                v = v + into[e].astype(F32)
-            fin[e] = v.astype(BF16)
+                arrived(into.at[e, rows], znr[e][h][half], neighbour[-sign])
+                v = v + into[e, rows].astype(F32)
+            fin[e, rows] = v.astype(BF16)
 
     wsr = [(rr.at[take("r")], rr.at[take("r")]) for _ in range(4)]
 
@@ -377,33 +404,40 @@
         wgq[0, zs] = query_grads(zs, xb)
         save.append(local(wgq.at[0, zs], gq_out.at[rows_out(zs, qb)]))
 
-    f1r = rr.at[take("r")]
-
-    def final0(start):
-        @pl.when(own)
-        def _():
-            keep(fin.at[0], hg_out.at[0], start)
-
-        @pl.when(jnp.logical_not(own))
-        def _():
-            swap(fin.at[0], hg_out.at[0], start)
-
-    stage0(False)
-    gather_first(0)
-    gather_second(0)
-    gather_third(0)
-    arrived(X.at[1, held, zh], s1r, swap1)
-    gather_first(1)
+    f1r = [rr.at[take("r")] for _ in (0, 1)]
+
+    def final0(h, start):
+        swap(fin.at[0], hg_out.at[0], hg_out.at[0], h, start)
+
+    for h in (0, 1):
+        stage0(h, False)
+        gather_first(0, h)
+    arrived(relay, s1r, mirror)
+    stage1(True)
+    gather_second(0, 0)
+    gather_second(0, 1)
+    gather_third(0, 0)
+    gather_third(0, 1)
+    stage1(False)
+    gather_first(1, 0)
+    gather_first(1, 1)
     load_wq.wait()
     load_wkv.wait()
     arrived(Wq.at[1 - xb], wr[0], pair)
     arrived(Wkv.at[1 - xb], wr[1], pair)
     project_held(0)
-    project_shared(0)
+    for k in (0, -1):
+        shared(0, k)
+        project(0, 1 - held, up(zh, k))
+    gather_second(1, 0)
+    gather_second(1, 1)
+    for k in (1, 2):
+        shared(0, k)
+        project(0, 1 - held, up(zh, k))
     send_partial(0)
-    gather_second(1)
+    gather_third(1, 0)
+    gather_third(1, 1)
     send_kv(0)
-    gather_third(1)
     attend(0)
     project_held(1)
     send_gkv(0)
@@ -412,23 +446,38 @@
     take_g(0)
     fars(0)
     send_kv(1)
-    scatter_own(0, 0)
+    scatter_own(0, 0, 0)
+    scatter_own(0, 1, 0)
     attend(1)
-    scatter_own(0, 1)
-    scatter_own(0, 2)
+    scatter_own(0, 0, 1)
+    scatter_own(0, 1, 1)
     send_gkv(1)
-    scatter_own(0, 3)
-    final0(True)
+    scatter_own(0, 0, 2)
+    scatter_own(0, 1, 2)
     take_g(1)
     fars(1)
-    for zs in range(4):
-        weight_grads_pair(zs)
-        scatter_own(1, zs)
-    send(fin.at[1], hg_out.at[1], f1r, swap1)
-    for zs in range(4):
-        weight_grads_own(zs)
-    final0(False)
-    arrived(hg_out.at[1], f1r, swap1)
+    for h in (0, 1):
+        scatter_own(0, h, 3)
+        final0(h, True)
+    weight_grads_pair(0)
+    weight_grads_pair(1)
+    scatter_own(1, 0, 0)
+    scatter_own(1, 1, 0)
+    weight_grads_pair(2)
+    weight_grads_pair(3)
+    for i in (1, 2):
+        for h in (0, 1):
+            scatter_own(1, h, i)
+    weight_grads_own(0)
+    weight_grads_own(1)
+    for h in (0, 1):
+        scatter_own(1, h, 3)
+        send(fin.at[1, part(h)], hg_out.at[1, part(h)], f1r[h], swap1)
+    weight_grads_own(2)
+    weight_grads_own(3)
+    for h in (0, 1):
+        final0(h, False)
+        arrived(hg_out.at[1, part(h)], f1r[h], swap1)
     arrived(att_out.at[1], ar, mirror)
     for zs in range(4):
         rows = rows_out(zs, 1 - qb)
@@ -440,6 +489,13 @@
         copy.wait_send()
 
 
+def finish(att, hg, gq, gkv, att_out, hg_out, gq_out, gkv_out):
+    att_out[...] = att[...]
+    hg_out[...] = hg[...]
+    gq_out[...] = gq[...].astype(F32)
+    gkv_out[...] = gkv[...].astype(F32)
+
+
 def rope_tables():
     freqs = 10000.0 ** (-2.0 * np.arange(HEAD // 2) / HEAD)
     angles = np.arange(TOK, dtype=np.float32)[:, None] * freqs.astype(np.float32)[None, :]
@@ -458,7 +514,7 @@
     big = V((2, 4, TOK, FEAT), BF16)
     mid = V((2, TOK, FEAT), BF16)
     scratch = [
-        V((2, 2, 4, TOK, FEAT), BF16),
+        V((2, 2, 4, TOK, FEAT), BF16), V((TOK, FEAT), BF16),
         V((2, QUARTER, 256), BF16), V((2, 64, QUARTER), BF16),
         V((2, TOK, 256), BF16), V((1, TOK), jnp.int32),
         V((2, 2, 2, TOK, 256), F32), V((2, 2, TOK, 128), F32), V((2, 2, 2, 128, 128), F32),
@@ -471,9 +527,9 @@
         big, big,
         mid, mid, mid, mid, mid, mid, mid,
         V((2, 4, FEAT, 256), BF16), V((4, 2, 64, FEAT), BF16),
-        pltpu.SemaphoreType.DMA((112,)),
-        pltpu.SemaphoreType.DMA((96,)),
-        pltpu.SemaphoreType.DMA((2, 2, 4, 2)),
+        pltpu.SemaphoreType.DMA((160,)),
+        pltpu.SemaphoreType.DMA((128,)),
+        pltpu.SemaphoreType.DMA((2, 2, 2, 4, 2)),
         pltpu.SemaphoreType.DMA((32,)),
     ]
     att, hg, gq, gkv = pl.pallas_call(
@@ -491,7 +547,27 @@
             collective_id=0, has_side_effects=True, vmem_limit_bytes=60 * 2**20
         ),
     )(hidden[0], query_weight[0], keyval_weight[0].swapaxes(1, 2), doc_ids[0], cotangent[0], cosf, sinf)
-    return att[None], hg[None], gq.astype(F32)[None], gkv.astype(F32).T[None]
+    steps = 4
+    specs = (
+        pl.BlockSpec((2, TOK // steps, 256), lambda i: (0, i, 0)),
+        pl.BlockSpec((2, TOK // steps, FEAT), lambda i: (0, i, 0)),
+        pl.BlockSpec((4096 // steps, 256), lambda i: (i, 0)),
+        pl.BlockSpec((64, 4096 // steps), lambda i: (0, i)),
+    )
+    att, hg, gq, gkv = pl.pallas_call(
+        finish,
+        grid=(steps,),
+        out_shape=(
+            jax.ShapeDtypeStruct(att.shape, BF16),
+            jax.ShapeDtypeStruct(hg.shape, BF16),
+            jax.ShapeDtypeStruct(gq.shape, F32),
+            jax.ShapeDtypeStruct(gkv.shape, F32),
+        ),
+        in_specs=list(specs),
+        out_specs=specs,
+        compiler_params=pltpu.CompilerParams(vmem_limit_bytes=60 * 2**20),
+    )(att, hg, gq, gkv)
+    return att[None], hg[None], gq[None], gkv.T[None]
 
 
 def solution(mesh):

time: 173 us -> 168 us (0.971)
  other arithmetic: 5.07 us -> 0 us
  Pallas kernels: 165 us -> 167 us
    broadcast_in_dim x2 -> x0, other arithmetic: 5.07 us -> none  [body(): return (att[None], hg[None], gq.astype(F32)[None], gkv.astype(F32).T[None])]
    pallas_call x0 -> x1, Pallas kernels: none -> 5.02 us  [body(): pl.pallas_call(finish, grid=(steps,), out_shape=(jax.ShapeDtypeStruct(att...]
    pallas_call x1, Pallas kernels: 165 us -> 162 us  [body(): pl.pallas_call(kernel, out_shape=(jax.ShapeDtypeStruct((2, TOK, 256), BF1...]
where the time goes in v4:
time: 168 us
  Pallas kernels  167 us (99%)
    pallas_call x1, Pallas kernels, body(): pl.pallas_call(kernel, out_shape=(jax.ShapeDtypeStruct((2, TOK, 256), BF1...  162 us
    pallas_call x1, Pallas kernels, body(): pl.pallas_call(finish, grid=(steps,), out_shape=(jax.ShapeDtypeStruct(att...  5.02 us

profile of v4, /device:TPU:31, one launch (start us, length us, event | category | flops | bytes accessed | tf_op | source)
XLA Modules:
  0.0 167.7 jit_solution(10154548936334818881)
XLA Ops:
  0.6 162.0 %shard_map.102 = (bf16[2,256,256]{2,1,0:T(8,128)(2,1)}, bf16[2,256,512]{2,1,0:T(8,128)(2,1)}, bf16[4096,256]{1,0:T(8,128)(2,1)}, bf16[64,4096]{1,0:T(8,128)(2,1)}) custom-call(bf16[2,256,512]{2,1,0:T(8,128)(2,1)} %bitcast.15, bf16[2,4096,256]{2,1,0:T(8,128)(2,1)} %bitcast.13, bf16[2,64,4096]{2,1,0:T(8,128)(2,1)} %bitcast.14, s32[2,1,256]{2,1,0:T(1,128)} %bitcast.17, ...), custom_call_target="tpu_custom_call" | custom-call | tf_op jit(solution)/shard_map/pallas_call | solution.py:535
  162.7 5.0 %shard_map.103 = (bf16[2,256,256]{2,1,0:T(8,128)(2,1)}, bf16[2,256,512]{2,1,0:T(8,128)(2,1)}, f32[4096,256]{1,0:T(8,128)}, f32[64,4096]{1,0:T(8,128)}) custom-call(bf16[2,256,256]{2,1,0:T(8,128)(2,1)} %get-tuple-element.12.att, bf16[2,256,512]{2,1,0:T(8,128)(2,1)} %get-tuple-element.13.hg, bf16[4096,256]{1,0:T(8,128)(2,1)} %get-tuple-element.14.gq, ...), custom_call_target="tpu_custom_call" | custom-call | tf_op jit(solution)/shard_map/pallas_call | solution.py:557

commit v5 on v4

--- a/solution.py
+++ b/solution.py
@@ -416,22 +416,19 @@
     stage1(True)
     gather_second(0, 0)
     gather_second(0, 1)
-    gather_third(0, 0)
-    gather_third(0, 1)
     stage1(False)
     gather_first(1, 0)
     gather_first(1, 1)
+    gather_third(0, 0)
+    gather_third(0, 1)
     load_wq.wait()
     load_wkv.wait()
     arrived(Wq.at[1 - xb], wr[0], pair)
     arrived(Wkv.at[1 - xb], wr[1], pair)
     project_held(0)
-    for k in (0, -1):
-        shared(0, k)
-        project(0, 1 - held, up(zh, k))
     gather_second(1, 0)
     gather_second(1, 1)
-    for k in (1, 2):
+    for k in ORDER:
         shared(0, k)
         project(0, 1 - held, up(zh, k))
     send_partial(0)

time: 168 us -> 166 us (0.988); the launches traced: 168 us -> 164 us
  Pallas kernels: 167 us -> 163 us
    pallas_call x1, Pallas kernels: 162 us -> 158 us  [body(): pl.pallas_call(kernel, out_shape=(jax.ShapeDtypeStruct((2, TOK, 256), BF1...]
where the time goes in v5:
time: 166 us; the launch traced here: 164 us
  Pallas kernels  163 us (98%)
    pallas_call x1, Pallas kernels, body(): pl.pallas_call(kernel, out_shape=(jax.ShapeDtypeStruct((2, TOK, 256), BF1...  158 us
    pallas_call x1, Pallas kernels, body(): pl.pallas_call(finish, grid=(steps,), out_shape=(jax.ShapeDtypeStruct(att...  5.02 us

profile of v5, /device:TPU:31, one launch (start us, length us, event | category | flops | bytes accessed | tf_op | source)
XLA Modules:
  0.0 163.8 jit_solution(17597460269897565357)
XLA Ops:
  0.6 158.1 %shard_map.102 = (bf16[2,256,256]{2,1,0:T(8,128)(2,1)}, bf16[2,256,512]{2,1,0:T(8,128)(2,1)}, bf16[4096,256]{1,0:T(8,128)(2,1)}, bf16[64,4096]{1,0:T(8,128)(2,1)}) custom-call(bf16[2,256,512]{2,1,0:T(8,128)(2,1)} %bitcast.15, bf16[2,4096,256]{2,1,0:T(8,128)(2,1)} %bitcast.13, bf16[2,64,4096]{2,1,0:T(8,128)(2,1)} %bitcast.14, s32[2,1,256]{2,1,0:T(1,128)} %bitcast.17, ...), custom_call_target="tpu_custom_call" | custom-call | tf_op jit(solution)/shard_map/pallas_call | solution.py:532
  158.7 5.0 %shard_map.103 = (bf16[2,256,256]{2,1,0:T(8,128)(2,1)}, bf16[2,256,512]{2,1,0:T(8,128)(2,1)}, f32[4096,256]{1,0:T(8,128)}, f32[64,4096]{1,0:T(8,128)}) custom-call(bf16[2,256,256]{2,1,0:T(8,128)(2,1)} %get-tuple-element.12.att, bf16[2,256,512]{2,1,0:T(8,128)(2,1)} %get-tuple-element.13.hg, bf16[4096,256]{1,0:T(8,128)(2,1)} %get-tuple-element.14.gq, ...), custom_call_target="tpu_custom_call" | custom-call | tf_op jit(solution)/shard_map/pallas_call | solution.py:554

commit v6 on v5

--- a/solution.py
+++ b/solution.py
@@ -257,7 +257,7 @@
             arrived(rPkv.at[e, i], prk[e][i], square[i])
             piece = piece + rPkv[e, i].astype(F32)
         KV[e, zh] = piece.astype(BF16)
-        for o in (1, 2, 3):
+        for o in (2, 1, 3):
             send(KV.at[e, zh], KV.at[e, zh], kvr[e][o - 1], zto[o])
         q = Pq[e, zl, xb]
         for i in range(3):
@@ -302,7 +302,7 @@
             v = pack(v)
             gfp[e, i] = v
             gsb[e, i] = v.astype(BF16)
-        for o in (1, 2, 3):
+        for o in (2, 1, 3):
             send(gsb.at[e, up(zh, o)], grb.at[e, o - 1], gr[e][o - 1], zto[o])
         for i in range(3):
             send(Gq.at[e, zl, xb], Gq.at[e, zl, xb], xrq[e][i], square[i])

time: 166 us -> 165 us (level)
  no operation moved by 1% of the time
where the time goes in v6:
time: 165 us; the launch traced here: 164 us
  Pallas kernels  163 us (99%)
    pallas_call x1, Pallas kernels, body(): pl.pallas_call(kernel, out_shape=(jax.ShapeDtypeStruct((2, TOK, 256), BF1...  158 us
    pallas_call x1, Pallas kernels, body(): pl.pallas_call(finish, grid=(steps,), out_shape=(jax.ShapeDtypeStruct(att...  5.02 us

profile of v6, /device:TPU:31, one launch (start us, length us, event | category | flops | bytes accessed | tf_op | source)
XLA Modules:
  0.0 163.7 jit_solution(4296558247703853393)
XLA Ops:
  0.6 158.0 %shard_map.102 = (bf16[2,256,256]{2,1,0:T(8,128)(2,1)}, bf16[2,256,512]{2,1,0:T(8,128)(2,1)}, bf16[4096,256]{1,0:T(8,128)(2,1)}, bf16[64,4096]{1,0:T(8,128)(2,1)}) custom-call(bf16[2,256,512]{2,1,0:T(8,128)(2,1)} %bitcast.15, bf16[2,4096,256]{2,1,0:T(8,128)(2,1)} %bitcast.13, bf16[2,64,4096]{2,1,0:T(8,128)(2,1)} %bitcast.14, s32[2,1,256]{2,1,0:T(1,128)} %bitcast.17, ...), custom_call_target="tpu_custom_call" | custom-call | tf_op jit(solution)/shard_map/pallas_call | solution.py:532
  158.7 5.0 %shard_map.103 = (bf16[2,256,256]{2,1,0:T(8,128)(2,1)}, bf16[2,256,512]{2,1,0:T(8,128)(2,1)}, f32[4096,256]{1,0:T(8,128)}, f32[64,4096]{1,0:T(8,128)}) custom-call(bf16[2,256,256]{2,1,0:T(8,128)(2,1)} %get-tuple-element.12.att, bf16[2,256,512]{2,1,0:T(8,128)(2,1)} %get-tuple-element.13.hg, bf16[4096,256]{1,0:T(8,128)(2,1)} %get-tuple-element.14.gq, ...), custom_call_target="tpu_custom_call" | custom-call | tf_op jit(solution)/shard_map/pallas_call | solution.py:554
